TPU v7x, 32 devices: a whole 2x2x4 slice. The times are simulated.
32 devices in a mesh: dp: 8 (over z, y), chan: 4 (over x, core).
Axes of the slice: x: 2, y: 2, z: 4, core: 2. Of those that a mesh axis runs over, the one named last changes fastest.
Arguments:
- inputs: bfloat16 [3136, 2048], P('dp', 'chan'), may hold values from -6 to 6
- conv_one: bfloat16 [9, 32, 2048], P(None, None, 'chan'), may hold values from -0.375 to 0.375
- conv_two: bfloat16 [9, 32, 2048], P(None, None, 'chan'), may hold values from -0.375 to 0.375
- probe_one: bfloat16 [2048, 512], P('chan'), may hold values from -0.125 to 0.125
- probe_two: bfloat16 [2048, 512], P('chan'), may hold values from -0.125 to 0.125
Outputs:
- restored: bfloat16 [3136, 2048], P('dp', 'chan')
- triangle: float32 [512, 512], replicated
All inputs are finite; a program needn't handle non-finite values.
Results may differ from a plain program's by a relative error of at most 0.028.
Values may be sent and summed in bfloat16 or wider, within the bound.
A program may use at most 64 MiB of HBM per device.

v0:
```python
import math

import jax
import jax.numpy as jnp
from jax import lax
from jax.sharding import PartitionSpec as P

SIDE = 7


def convolve(field, weight):
    pixels, width = field.shape
    group_width = weight.shape[1]
    groups = width // group_width
    images = field.reshape(pixels // (SIDE * SIDE), SIDE, SIDE, width)
    padded = jnp.pad(images, ((0, 0), (1, 1), (1, 1), (0, 0)))
    total = jnp.zeros((pixels, groups, group_width), jnp.float32)
    for offset in range(9):
        row_shift = offset // 3
        col_shift = offset % 3
        window = padded[:, row_shift : row_shift + SIDE, col_shift : col_shift + SIDE, :]
        window = window.reshape(pixels, groups, group_width)
        kernel = weight[offset].reshape(group_width, groups, group_width)
        total = total + jnp.einsum(
            "pgi,igo->pgo", window, kernel, preferred_element_type=jnp.float32
        )
    return total.reshape(pixels, width).astype(jnp.bfloat16)


def gram_of(sketch):
    return lax.dot_general(
        sketch, sketch, (((0,), (0,)), ((), ())), preferred_element_type=jnp.float32
    )


def cross_of(sketch, responses):
    return lax.dot_general(
        sketch, responses, (((0,), (0,)), ((), ())), preferred_element_type=jnp.float32
    )


def finish(sketch, gram, cross):
    lower = jnp.linalg.cholesky(gram)
    coeffs = lax.linalg.triangular_solve(lower, cross, left_side=True, lower=True).astype(
        jnp.bfloat16
    )
    mapped = lax.linalg.triangular_solve(
        lower, coeffs.astype(jnp.float32), left_side=True, lower=True, transpose_a=True
    ).astype(jnp.bfloat16)
    return (jnp.dot(sketch, mapped, preferred_element_type=jnp.float32).astype(jnp.bfloat16), lower)


def compress(responses, probe):
    partial_sketch = jnp.dot(responses, probe, preferred_element_type=jnp.float32)
    sketch = lax.psum(partial_sketch, "chan").astype(jnp.bfloat16)
    gram, cross = lax.psum((gram_of(sketch), cross_of(sketch, responses)), "dp")
    return finish(sketch, gram, cross)


def per_device(inputs, conv_one, conv_two, probe_one, probe_two):
    responses_one = convolve(inputs, conv_one)
    restored_one, lower_one = compress(responses_one, probe_one)
    activated = jnp.maximum(restored_one, jnp.zeros((), jnp.bfloat16))
    responses_two = convolve(activated, conv_two)
    restored, lower_two = compress(responses_two, probe_two)
    total_rows = inputs.shape[0] * lax.axis_size("dp")
    triangle = jnp.transpose(lower_two) * (1.0 / math.sqrt(total_rows))
    return (restored, triangle)


def solution(mesh):
    in_specs = (
        P("dp", "chan"),
        P(None, None, "chan"),
        P(None, None, "chan"),
        P("chan", None),
        P("chan", None),
    )
    out_specs = (P("dp", "chan"), P())
    return jax.shard_map(
        per_device, mesh=mesh, in_specs=in_specs, out_specs=out_specs, check_vma=False
    )
```

profile of v0, /device:TPU:0, one launch (start us, length us, event | category | flops | bytes accessed | tf_op | source)
XLA Modules:
  0.0 632.3 jit_solution(13483223838432303768)
XLA Ops:
  9.8 1.7 pad_slice_fusion.8
  11.5 3.1 reshape.121
  15.3 2.1 reshape.120
  18.2 3.0 reshape.119
  21.9 2.2 reshape.123
  24.9 2.1 reshape.124
  27.7 2.1 reshape.125
  30.7 2.3 reshape.118
  33.1 2.1 reshape.126
  35.2 2.3 fusion.24
  45.9 21.3 %all-reduce.13 = bf16[392,512]{1,0:T(8,128)(2,1)S(1)} all-reduce(f32[392,512]{1,0:T(8,128)S(1)} %fusion.217), channel_id=1, replica_groups=mesh['dp'=8,'chan'=4] {'chan'}, use_global_device_ids=true, to_apply=%region_0.1 | all-reduce | flops 200704 | bytes 1204224 | tf_op jit(solution)/shard_map/psum | solution.py:55
  67.2 1.5 fusion.222
  68.7 1.5 fusion.223
  77.5 95.6 %all-reduce.12.cloned.1.call-done = (f32[512,512]{1,0:T(8,128)}, f32[512,512]{0,1:T(8,128)}) async-done(((f32[512,512]{1,0:T(8,128)}, f32[512,512]{0,1:T(8,128)}), (f32[512,512]{1,0:T(8,128)}, f32[512,512]{0,1:T(8,128)})) %all-reduce.12.cloned.1.call-update) | async-done | bytes 2097168 | tf_op jit(solution)/shard_map/psum | solution.py:56
  173.1 1.6 copy.60
  176.0 11.7 %cholesky.286 = f32[128,128]{1,0:T(8,128)S(1)} custom-call(f32[128,128]{1,0:T(8,128)S(1)} %cholesky.426), custom_call_target="Cholesky" | custom-call | tf_op jit(solution)/shard_map/jit(cholesky)/cholesky | solution.py:43
  187.9 9.8 %custom-call.31 = f32[1,128,128]{1,2,0:T(8,128)S(1)} custom-call(f32[1,128,128]{2,1,0:T(8,128)S(1)} %get-tuple-element.120), custom_call_target="InvertDiagBlocksLowerTriangular" | custom-call | tf_op jit(solution)/shard_map/jit(cholesky)/cholesky | solution.py:43
  198.9 1.3 convolution_subtract_fusion.13
  200.2 11.7 %cholesky.305 = f32[128,128]{1,0:T(8,128)S(1)} custom-call(f32[128,128]{1,0:T(8,128)S(1)} %cholesky.430), custom_call_target="Cholesky" | custom-call | tf_op jit(solution)/shard_map/jit(cholesky)/cholesky | solution.py:43
  212.0 10.0 %custom-call.32 = f32[1,128,128]{1,2,0:T(8,128)S(1)} custom-call(f32[1,128,128]{2,1,0:T(8,128)S(1)} %get-tuple-element.117), custom_call_target="InvertDiagBlocksLowerTriangular" | custom-call | tf_op jit(solution)/shard_map/jit(cholesky)/cholesky | solution.py:43
  222.2 1.3 convolution_subtract_fusion.15
  223.5 11.7 %cholesky.326 = f32[128,128]{1,0:T(8,128)S(1)} custom-call(f32[128,128]{1,0:T(8,128)S(1)} %cholesky.435), custom_call_target="Cholesky" | custom-call | tf_op jit(solution)/shard_map/jit(cholesky)/cholesky | solution.py:43
  236.0 9.8 %custom-call.33 = f32[1,128,128]{1,2,0:T(8,128)S(1)} custom-call(f32[1,128,128]{2,1,0:T(8,128)S(1)} %get-tuple-element.114), custom_call_target="InvertDiagBlocksLowerTriangular" | custom-call | tf_op jit(solution)/shard_map/jit(cholesky)/cholesky | solution.py:43
  247.2 11.9 %cholesky.343 = f32[128,128]{1,0:T(8,128)S(1)} custom-call(f32[128,128]{1,0:T(8,128)S(1)} %convolution_subtract_fusion.17), custom_call_target="Cholesky" | custom-call | tf_op jit(solution)/shard_map/jit(cholesky)/cholesky | solution.py:43
  263.3 8.5 %while.8 = (s32[]{:T(128)}, f32[512,512]{1,0:T(8,128)S(1)}, s32[4,2]{0,1:T(2,128)S(1)}, f32[4,128,128]{2,1,0:T(8,128)S(1)}, s32[]{:T(128)}) while((s32[]{:T(128)}, f32[512,512]{1,0:T(8,128)S(1)}, s32[4,2]{0,1:T(2,128)S(1)}, f32[4,128,128]{2,1,0:T(8,128)S(1)}, s32[]{:T(128)}) %tuple.96), condition=%wide.while_cond.1, body=%wide.while_body.1.sunk | while | flops 2 | bytes 131181 | solution.py:47
  264.0 1.4 bitcast_dynamic-update-slice_fusion.4
  266.1 1.4 bitcast_dynamic-update-slice_fusion.4
  268.2 1.4 bitcast_dynamic-update-slice_fusion.4
  270.3 1.4 bitcast_dynamic-update-slice_fusion.4
  271.8 39.3 %custom-call.35 = f32[4,128,128]{1,2,0:T(8,128)S(1)} custom-call(f32[4,128,128]{2,1,0:T(8,128)S(1)} %get-tuple-element.34), custom_call_target="InvertDiagBlocksLowerTriangular" | custom-call | tf_op jit(solution)/shard_map/triangular_solve/custom-call.8 | solution.py:47
  311.1 1.4 fusion.146
  312.5 1.3 convolution_subtract_fusion.7
  320.1 1.4 pad_slice_fusion
  321.5 3.0 reshape.130
  324.5 3.4 reshape.129
  327.9 2.2 reshape.134
  330.0 2.1 reshape.133
  332.2 2.1 reshape.131
  334.2 2.1 reshape.135
  337.2 2.1 reshape.136
  339.3 2.3 fusion.10
  350.3 19.6 %all-reduce.14 = bf16[392,512]{1,0:T(8,128)(2,1)S(1)} all-reduce(f32[392,512]{1,0:T(8,128)S(1)} %fusion.219), channel_id=1, replica_groups=mesh['dp'=8,'chan'=4] {'chan'}, use_global_device_ids=true, to_apply=%region_11.15 | all-reduce | flops 200704 | bytes 1204224 | tf_op jit(solution)/shard_map/psum | solution.py:55
  369.9 1.5 fusion.220
  371.4 1.5 fusion.221
  372.9 101.9 %all-reduce.10.cloned.1.call-done = (f32[512,512]{1,0:T(8,128)}, f32[512,512]{0,1:T(8,128)}) async-done(((f32[512,512]{1,0:T(8,128)}, f32[512,512]{0,1:T(8,128)}), (f32[512,512]{1,0:T(8,128)}, f32[512,512]{0,1:T(8,128)})) %all-reduce.10.cloned.1.call-update) | async-done | bytes 2097168 | tf_op jit(solution)/shard_map/psum | solution.py:56
  474.8 1.6 copy.80
  477.7 11.7 %cholesky.358 = f32[128,128]{1,0:T(8,128)S(1)} custom-call(f32[128,128]{1,0:T(8,128)S(1)} %cholesky.439), custom_call_target="Cholesky" | custom-call | tf_op jit(solution)/shard_map/jit(cholesky)/cholesky | solution.py:43
  489.6 9.8 %custom-call.36 = f32[1,128,128]{1,2,0:T(8,128)S(1)} custom-call(f32[1,128,128]{2,1,0:T(8,128)S(1)} %get-tuple-element.110), custom_call_target="InvertDiagBlocksLowerTriangular" | custom-call | tf_op jit(solution)/shard_map/jit(cholesky)/cholesky | solution.py:43
  500.7 1.3 convolution_subtract_fusion.12
  501.9 11.7 %cholesky.377 = f32[128,128]{1,0:T(8,128)S(1)} custom-call(f32[128,128]{1,0:T(8,128)S(1)} %cholesky.443), custom_call_target="Cholesky" | custom-call | tf_op jit(solution)/shard_map/jit(cholesky)/cholesky | solution.py:43
  515.0 10.0 %custom-call.37 = f32[1,128,128]{1,2,0:T(8,128)S(1)} custom-call(f32[1,128,128]{2,1,0:T(8,128)S(1)} %get-tuple-element.107), custom_call_target="InvertDiagBlocksLowerTriangular" | custom-call | tf_op jit(solution)/shard_map/jit(cholesky)/cholesky | solution.py:43
  525.3 1.3 convolution_subtract_fusion.14
  526.6 11.7 %cholesky.398 = f32[128,128]{1,0:T(8,128)S(1)} custom-call(f32[128,128]{1,0:T(8,128)S(1)} %cholesky.448), custom_call_target="Cholesky" | custom-call | tf_op jit(solution)/shard_map/jit(cholesky)/cholesky | solution.py:43
  538.9 9.8 %custom-call.38 = f32[1,128,128]{1,2,0:T(8,128)S(1)} custom-call(f32[1,128,128]{2,1,0:T(8,128)S(1)} %get-tuple-element.104), custom_call_target="InvertDiagBlocksLowerTriangular" | custom-call | tf_op jit(solution)/shard_map/jit(cholesky)/cholesky | solution.py:43
  550.2 11.9 %cholesky.415 = f32[128,128]{1,0:T(8,128)S(1)} custom-call(f32[128,128]{1,0:T(8,128)S(1)} %convolution_subtract_fusion.16), custom_call_target="Cholesky" | custom-call | tf_op jit(solution)/shard_map/jit(cholesky)/cholesky | solution.py:43
  566.5 8.5 %while.9 = (s32[]{:T(128)}, f32[512,512]{1,0:T(8,128)S(1)}, s32[4,2]{0,1:T(2,128)S(1)}, f32[4,128,128]{2,1,0:T(8,128)S(1)}, s32[]{:T(128)}) while((s32[]{:T(128)}, f32[512,512]{1,0:T(8,128)S(1)}, s32[4,2]{0,1:T(2,128)S(1)}, f32[4,128,128]{2,1,0:T(8,128)S(1)}, s32[]{:T(128)}) %tuple.108), condition=%wide.while_cond.1.clone, body=%wide.while_body.1.clone.sunk | while | flops 2 | bytes 131181 | solution.py:47
  567.2 1.4 bitcast_dynamic-update-slice_fusion.5
  569.3 1.4 bitcast_dynamic-update-slice_fusion.5
  571.4 1.4 bitcast_dynamic-update-slice_fusion.5
  573.6 1.4 bitcast_dynamic-update-slice_fusion.5
  575.0 39.3 %custom-call.40 = f32[4,128,128]{1,2,0:T(8,128)S(1)} custom-call(f32[4,128,128]{2,1,0:T(8,128)S(1)} %get-tuple-element.36), custom_call_target="InvertDiagBlocksLowerTriangular" | custom-call | tf_op jit(solution)/shard_map/triangular_solve/custom-call.8 | solution.py:47
  614.3 1.4 fusion.141
  615.7 1.3 convolution_subtract_fusion.3
  623.8 1.3 copy.81
  (214 shorter events, 65.4 us)
Async XLA Ops:
  7.2 38.3 %copy-start = (bf16[512,512]{1,0:T(8,128)(2,1)S(1)}, bf16[512,512]{1,0:T(8,128)(2,1)}, u32[]{:S(2)}) copy-start(bf16[512,512]{1,0:T(8,128)(2,1)} %param.13) | copy-start | bytes 1572868
  7.2 2.5 copy-start.40
  7.2 165.9 %all-reduce.12.cloned.1.call-start = ((), (), s32[]{:S(2)}) async-start(), calls=%async_computation.1 | async-start | bytes 4194304 | tf_op jit(solution)/shard_map/psum | solution.py:56
  11.5 3.8 copy-start.20
  17.5 4.5 copy-start.19
  35.2 2.3 copy-start.2
  35.2 2.3 copy-start.33
  37.5 1.4 copy-start.5
  37.5 1.4 copy-start.34
  38.3 1.6 copy-start.6
  38.3 1.6 copy-start.35
  39.7 1.5 copy-start.7
  39.7 1.5 copy-start.36
  40.7 1.6 copy-start.8
  40.7 1.6 copy-start.37
  42.0 1.0 copy-start.39
  43.3 1.4 copy-start.3
  68.7 1.9 copy-start.41
  70.2 404.7 %all-reduce.10.cloned.1.call-start = ((), (), s32[]{:S(2)}) async-start(), calls=%async_computation | async-start | bytes 4194304 | tf_op jit(solution)/shard_map/psum | solution.py:56
  173.1 1.7 copy-start.14
  175.0 1.0 copy-start.18
  263.2 51.0 %copy-start.22 = (f32[512,512]{1,0:T(8,128)S(1)}, f32[512,512]{1,0:T(8,128)}, u32[]{:S(2)}) copy-start(f32[512,512]{1,0:T(8,128)} %get-tuple-element.59) | copy-start | bytes 3145732
  321.5 6.4 %copy-start.21 = (bf16[8,7,7,512]{3,2,1,0:T(8,128)(2,1)S(1)}, bf16[8,7,7,512]{3,2,1,0:T(8,128)(2,1)}, u32[]{:S(2)}) copy-start(bf16[8,7,7,512]{3,2,1,0:T(8,128)(2,1)} %get-tuple-element.72) | copy-start | bytes 1204228
  336.3 3.0 copy-start.32
  339.3 2.3 copy-start.13
  339.3 2.4 copy-start.31
  341.7 1.4 copy-start.12
  341.7 1.4 copy-start.30
  342.5 1.6 copy-start.11
  342.5 1.6 copy-start.29
  343.9 1.5 copy-start.10
  343.9 1.5 copy-start.28
  344.8 1.6 copy-start.9
  344.8 1.6 copy-start.27
  346.1 1.0 copy-start.38
  346.4 1.1 copy-start.24
  347.4 1.4 copy-start.4
  347.4 1.4 copy-start.26
  348.8 1.0 copy-start.25
  474.8 1.7 copy-start.15
  476.7 1.0 copy-start.17
  566.5 50.9 %copy-start.23 = (f32[512,512]{1,0:T(8,128)S(1)}, f32[512,512]{1,0:T(8,128)}, u32[]{:S(2)}) copy-start(f32[512,512]{1,0:T(8,128)} %get-tuple-element.57) | copy-start | bytes 3145732
  622.2 1.5 copy-start.16
  622.6 2.5 copy-start.1
Sparse Core Ops, SparseCore 0:
  70.3 102.7 all-reduce.11
  373.0 101.7 all-reduce.9
where the time goes:
time: 640 us; the launch traced here: 632 us
  other arithmetic  239 us (37%)
  waiting for transfers between devices  198 us (31%)
  local copies, waits for them, and re-layouts  82.1 us (13%)
  matrix products  51.7 us (8%)
  blocking collectives  40.9 us (6%)
  between operations  20.5 us (3%)
    psum x2, waiting for transfers between devices, compress(): gram, cross = lax.psum((gram_of(sketch), cross_of(sketch, responses)), 'dp')  198 us
    another operation x29, other arithmetic, finish(): lower = jnp.linalg.cholesky(gram)  158 us
    another operation x4, other arithmetic, finish(): lax.linalg.triangular_solve(lower, coeffs.astype(jnp.float32), left_side=...  78.8 us
    psum x2, blocking collectives, compress(): sketch = lax.psum(partial_sketch, 'chan').astype(jnp.bfloat16)  40.9 us
    reshape x16, local copies, waits for them, and re-layouts, convolve(): window = window.reshape(pixels, groups, group_width)  36.8 us
    another operation x27, local copies, waits for them, and re-layouts, finish(): lax.linalg.triangular_solve(lower, coeffs.astype(jnp.float32), left_side=...  16.8 us
    dot_general x18, matrix products, convolve(): jnp.einsum('pgi,igo->pgo', window, kernel, preferred_element_type=jnp.flo...  16.6 us
  transfers between devices with their start and end apart: 2, of which 2 were waited for; matrix products, arithmetic and copies ran while one was open for 1% of the time, Pallas kernels for 0%

commit v1 on v0

v1 whole, which is shorter than its diff:
```python
import functools
import math

import jax
import jax.numpy as jnp
from jax import lax
from jax.experimental import pallas as pl
from jax.experimental.pallas import tpu as pltpu
from jax.sharding import PartitionSpec as P

SIDE = 7
PAD = 16
BLOCK = 128
PANEL = 16
F32 = jnp.float32
BF16 = jnp.bfloat16
VMEM_LIMIT = 48 * 1024 * 1024


def dot_f32(a, b, dims):
    return lax.dot_general(
        a, b, (dims, ((), ())), preferred_element_type=F32, precision=lax.Precision.HIGHEST
    )


def dot_bf16(a, b, dims):
    return lax.dot_general(a, b, (dims, ((), ())), preferred_element_type=F32)


def conv_into(field_ref, weight_ref, pad_ref, out_ref):
    rows, width = field_ref.shape
    group = weight_ref.shape[1]
    lanes = min(256, width)
    pad_ref[0:PAD, :] = jnp.zeros((PAD, width), F32)
    pad_ref[PAD + rows : PAD + rows + PAD, :] = jnp.zeros((PAD, width), F32)
    pad_ref[PAD : PAD + rows, :] = field_ref[...].astype(F32)
    place = lax.broadcasted_iota(jnp.int32, (rows, lanes), 0).astype(F32)
    pixel = place - (SIDE * SIDE) * jnp.floor((place + 0.5) * (1.0 / (SIDE * SIDE)))
    line = jnp.floor((pixel + 0.5) * (1.0 / SIDE))
    column = pixel - SIDE * line
    one, zero = jnp.ones((), F32), jnp.zeros((), F32)
    line_ok = (jnp.where(line > 0.5, one, zero), None, jnp.where(line < SIDE - 1.5, one, zero))
    column_ok = (jnp.where(column > 0.5, one, zero), None, jnp.where(column < SIDE - 1.5, one, zero))
    same = (
        lax.broadcasted_iota(jnp.int32, (lanes, lanes), 0) // group
        == lax.broadcasted_iota(jnp.int32, (lanes, lanes), 1) // group
    )
    for start in range(0, width, lanes):
        total = None
        for a in range(3):
            for b in range(3):
                shift = (a - 1) * SIDE + (b - 1)
                window = pad_ref[PAD + shift : PAD + shift + rows, start : start + lanes]
                if line_ok[a] is not None:
                    window = window * line_ok[a]
                if column_ok[b] is not None:
                    window = window * column_ok[b]
                small = weight_ref[3 * a + b, :, start : start + lanes]
                full = jnp.concatenate([small] * (lanes // group), axis=0)
                full = jnp.where(same, full, jnp.zeros((), BF16))
                part = dot_bf16(window.astype(BF16), full, ((1,), (0,)))
                total = part if total is None else total + part
        out_ref[:, start : start + lanes] = total.astype(BF16)


def split3(x):
    high = x.astype(BF16)
    rest = x - high.astype(F32)
    middle = rest.astype(BF16)
    low = (rest - middle.astype(F32)).astype(BF16)
    return high, middle, low


def eliminate_block(work_ref):
    row_of = lax.broadcasted_iota(jnp.int32, (PANEL, BLOCK), 0)
    for panel in range(BLOCK // PANEL):
        top = panel * PANEL
        left = work_ref[top : top + PANEL, 0:BLOCK]
        right = work_ref[top : top + PANEL, BLOCK : 2 * BLOCK]
        cols = [
            jnp.broadcast_to(left[:, top + k : top + k + 1], (PANEL, BLOCK)) for k in range(PANEL)
        ]
        scale = jnp.zeros((PANEL, BLOCK), F32)
        for i in range(PANEL):
            pivot = jnp.broadcast_to(cols[i][i : i + 1, :], (PANEL, BLOCK))
            root = lax.rsqrt(pivot)
            root = root * (1.5 - 0.5 * pivot * root * root)
            scale = jnp.where(row_of == i, root, scale)
            if i < PANEL - 1:
                factor = jnp.where(row_of > i, cols[i] * (root * root), 0.0)
                for k in range(i + 1, PANEL):
                    cols[k] = cols[k] - factor * cols[k][i : i + 1, :]
                left = left - factor * left[i : i + 1, :]
                right = right - factor * right[i : i + 1, :]
        left = left * scale
        right = right * scale
        lane_of = lax.broadcasted_iota(jnp.int32, (PANEL, BLOCK), 1)
        left = jnp.where(lane_of >= top + row_of, left, 0.0)
        work_ref[top : top + PANEL, 0:BLOCK] = left
        work_ref[top : top + PANEL, BLOCK : 2 * BLOCK] = right
        if top + PANEL < BLOCK:
            rest = top + PANEL
            h, m, l = split3(left)
            hr, mr, lr = split3(right)
            first = jnp.concatenate([h, h, m, h, l, m], axis=0)
            second = jnp.concatenate(
                [
                    jnp.concatenate([h, m, h, l, h, m], axis=0),
                    jnp.concatenate([hr, mr, hr, lr, hr, mr], axis=0),
                ],
                axis=1,
            )
            update = dot_bf16(first, second, ((0,), (0,)))
            work_ref[rest:BLOCK, :] = work_ref[rest:BLOCK, :] - update[rest:BLOCK, :]


def eliminate(big_ref, work_ref, size):
    blocks = size // BLOCK
    square = (BLOCK, BLOCK)
    eye = jnp.where(
        lax.broadcasted_iota(jnp.int32, square, 0) == lax.broadcasted_iota(jnp.int32, square, 1),
        1.0,
        0.0,
    )

    @pl.loop(0, blocks)
    def _(b):
        at = pl.ds(pl.multiple_of(b * BLOCK, BLOCK), BLOCK)
        work_ref[:, 0:BLOCK] = big_ref[at, at]
        work_ref[:, BLOCK : 2 * BLOCK] = eye
        eliminate_block(work_ref)
        inverse = work_ref[:, BLOCK : 2 * BLOCK]
        big_ref[at, :] = dot_f32(inverse, big_ref[at, :], ((1,), (0,)))
        big_ref[at, at] = work_ref[:, 0:BLOCK]

        @pl.loop(b + 1, blocks)
        def _(other):
            to = pl.ds(pl.multiple_of(other * BLOCK, BLOCK), BLOCK)
            big_ref[to, :] = big_ref[to, :] - dot_f32(big_ref[at, to], big_ref[at, :], ((0,), (0,)))


def solve_into(gram_ref, cross_ref, mapped_ref, upper_ref, big_ref, work_ref):
    size = gram_ref.shape[0]
    square = (size, size)
    row_of = lax.broadcasted_iota(jnp.int32, square, 0)
    lane_of = lax.broadcasted_iota(jnp.int32, square, 1)
    big_ref[:, 0:size] = gram_ref[...]
    big_ref[:, size : 2 * size] = jnp.where(row_of == lane_of, 1.0, 0.0)
    eliminate(big_ref, work_ref, size)
    if upper_ref is not None:
        upper_ref[...] = jnp.where(lane_of >= row_of, big_ref[:, 0:size], 0.0)
    inverse = big_ref[:, size : 2 * size]
    coeffs = dot_f32(cross_ref[...], inverse, ((1,), (1,))).astype(BF16)
    mapped_ref[...] = dot_f32(coeffs.astype(F32), inverse, ((1,), (0,))).astype(BF16)


def conv_kernel(field_ref, weight_ref, probe_ref, responses_ref, partial_ref, pad_ref):
    conv_into(field_ref, weight_ref, pad_ref, responses_ref)
    partial_ref[...] = dot_bf16(responses_ref[...], probe_ref[...], ((1,), (0,)))


def conv_call(field, weight, probe):
    rows, width = field.shape
    return pl.pallas_call(
        conv_kernel,
        out_shape=(
            jax.ShapeDtypeStruct((rows, width), BF16),
            jax.ShapeDtypeStruct((rows, probe.shape[1]), F32),
        ),
        scratch_shapes=[pltpu.VMEM((rows + 2 * PAD, width), F32)],
        compiler_params=pltpu.CompilerParams(vmem_limit_bytes=VMEM_LIMIT),
    )(field, weight, probe)


def solve_call(gram, cross):
    size = gram.shape[0]
    return pl.pallas_call(
        solve_into,
        out_shape=(
            jax.ShapeDtypeStruct(cross.shape, BF16),
            jax.ShapeDtypeStruct(gram.shape, F32),
        ),
        scratch_shapes=[pltpu.VMEM((size, 2 * size), F32), pltpu.VMEM((BLOCK, 2 * BLOCK), F32)],
        compiler_params=pltpu.CompilerParams(vmem_limit_bytes=VMEM_LIMIT),
    )(gram, cross)


def layer(field, weight, probe):
    responses, partial = conv_call(field, weight, probe)
    sketch = lax.psum(partial, "chan").astype(BF16)
    gram = dot_bf16(sketch, sketch, ((0,), (0,)))
    cross = dot_bf16(responses, sketch, ((0,), (0,)))
    gram = lax.psum(gram, "dp")
    cross = lax.psum_scatter(cross, "dp", scatter_dimension=0, tiled=True)
    mapped, upper = solve_call(gram, cross)
    mapped = lax.all_gather(mapped, "dp", axis=0, tiled=True)
    return dot_bf16(sketch, mapped, ((1,), (1,))).astype(BF16), upper


def per_device(inputs, conv_one, conv_two, probe_one, probe_two):
    restored_one, _ = layer(inputs, conv_one, probe_one)
    activated = jnp.maximum(restored_one, jnp.zeros((), BF16))
    restored, upper = layer(activated, conv_two, probe_two)
    total_rows = inputs.shape[0] * lax.axis_size("dp")
    return (restored, upper * (1.0 / math.sqrt(total_rows)))


def solution(mesh):
    in_specs = (
        P("dp", "chan"),
        P(None, None, "chan"),
        P(None, None, "chan"),
        P("chan", None),
        P("chan", None),
    )
    return jax.shard_map(
        per_device, mesh=mesh, in_specs=in_specs, out_specs=(P("dp", "chan"), P()), check_vma=False
    )
```

time: 640 us -> 475 us (0.74); the launches traced: 632 us -> 474 us
  other arithmetic: 239 us -> 1.08 us
  waiting for transfers between devices: 198 us -> 286 us
  local copies, waits for them, and re-layouts: 82.1 us -> 7.95 us
  blocking collectives: 40.9 us -> 103 us
  Pallas kernels: 0 us -> 54.3 us
  matrix products: 51.7 us -> 7.41 us
  between operations: 20.5 us -> 13.8 us
    another operation x33 -> x0, other arithmetic: 237 us -> none  [the longest x29 158 us: finish(): lower = jnp.linalg.cholesky(gram)]
    reduce_scatter x0 -> x2, waiting for transfers between devices: none -> 133 us  [layer(): cross = lax.psum_scatter(cross, 'dp', scatter_dimension=0, tiled=True)]
    all_gather x0 -> x2, blocking collectives: none -> 63.1 us  [layer(): mapped = lax.all_gather(mapped, 'dp', axis=0, tiled=True)]
    pallas_call x0 -> x4, Pallas kernels: none -> 54.3 us  [the longest x2 51 us: solve_call(): pl.pallas_call(solve_into, out_shape=(jax.ShapeDtypeStruct(cross.shape, B...]
    psum x2, waiting for transfers between devices: 198 us -> 152 us  [layer(): gram = lax.psum(gram, 'dp')]
    reshape x18 -> x0, local copies, waits for them, and re-layouts: 38.1 us -> none  [the longest x16 36.8 us: convolve(): window = window.reshape(pixels, groups, group_width)]
    another operation x40 -> x0, matrix products: 27 us -> none  [the longest x12 10.9 us: finish(): lower = jnp.linalg.cholesky(gram)]
    dot_general x26 -> x6, matrix products: 24.7 us -> 7.41 us  [dot_bf16(): return lax.dot_general(a, b, (dims, ((), ())), preferred_element_type=F32)]
  transfers between devices with their start and end apart: 2 -> 4, of which waited for: 2 -> 4; matrix products, arithmetic and copies ran while one was open for 1% -> 1% of each run, Pallas kernels for 0% -> 0%
where the time goes in v1:
time: 475 us; the launch traced here: 474 us
  waiting for transfers between devices  286 us (60%)
  blocking collectives  103 us (22%)
  Pallas kernels  54.3 us (11%)
  between operations  13.8 us (3%)
  local copies, waits for them, and re-layouts  7.95 us (2%)
  matrix products  7.41 us (2%)
    psum x2, waiting for transfers between devices, layer(): gram = lax.psum(gram, 'dp')  152 us
    reduce_scatter x2, waiting for transfers between devices, layer(): cross = lax.psum_scatter(cross, 'dp', scatter_dimension=0, tiled=True)  133 us
    all_gather x2, blocking collectives, layer(): mapped = lax.all_gather(mapped, 'dp', axis=0, tiled=True)  63.1 us
    pallas_call x2, Pallas kernels, solve_call(): pl.pallas_call(solve_into, out_shape=(jax.ShapeDtypeStruct(cross.shape, B...  51 us
    psum x2, blocking collectives, layer(): sketch = lax.psum(partial, 'chan').astype(BF16)  40.4 us
  transfers between devices with their start and end apart: 4, of which 4 were waited for; matrix products, arithmetic and copies ran while one was open for 1% of the time, Pallas kernels for 0%

profile of v1, /device:TPU:0, one launch (start us, length us, event | category | flops | bytes accessed | tf_op | source)
XLA Modules:
  0.0 474.4 jit_solution(14972177731904221375)
XLA Ops:
  7.2 0.0 all-reduce.5.cloned.1.call-start
  7.2 0.0 copy-start.2
  7.2 1.0 copy-done.2
  8.3 0.0 copy-start.4
  8.3 1.0 copy-done.4
  9.3 0.0 copy-start.5
  9.3 1.0 copy-done.5
  10.2 1.6 shard_map.68
  11.9 21.3 %all-reduce.8 = bf16[392,512]{1,0:T(8,128)(2,1)S(1)} all-reduce(f32[392,512]{1,0:T(8,128)S(1)} %get-tuple-element.9), channel_id=1, replica_groups=mesh['dp'=8,'chan'=4] {'chan'}, use_global_device_ids=true, to_apply=%region_0.0 | all-reduce | flops 200704 | bytes 1204224 | tf_op jit(solution)/shard_map/psum | solution.py:190
  33.2 1.4 fusion.14
  34.6 0.0 all-reduce.5.cloned.1.call-update
  34.6 0.0 reduce-scatter.3.cloned.1.call-start
  34.7 1.5 fusion.13
  36.2 0.0 reduce-scatter.3.cloned.1.call-update
  36.2 0.0 all-reduce.7.cloned.1.call-start
  36.3 77.2 %all-reduce.5.cloned.1.call-done.gram_ref = f32[512,512]{1,0:T(8,128)} async-done(((f32[512,512]{1,0:T(8,128)}), f32[512,512]{1,0:T(8,128)}) %all-reduce.5.cloned.1.call-update) | async-done | bytes 1048592 | tf_op jit(solution)/shard_map/psum | solution.py:193
  113.4 66.9 %reduce-scatter.3.cloned.1.call-done.cross_ref = f32[64,512]{1,0:T(8,128)} async-done(((f32[512,512]{1,0:T(8,128)}), f32[64,512]{1,0:T(8,128)}) %reduce-scatter.3.cloned.1.call-update) | async-done | bytes 131088 | tf_op jit(solution)/shard_map/reduce_scatter | solution.py:194
  180.3 0.0 copy-start
  180.3 1.2 copy-done
  181.5 0.0 copy-start.7
  181.5 0.9 copy-done.7
  182.4 25.9 %shard_map.69 = (bf16[64,512]{1,0:T(8,128)(2,1)S(1)}, f32[512,512]{1,0:T(8,128)}) custom-call(f32[512,512]{1,0:T(8,128)S(1)} %copy-done, f32[64,512]{1,0:T(8,128)S(1)} %copy-done.7), custom_call_target="tpu_custom_call" | custom-call | tf_op jit(solution)/shard_map/pallas_call | solution.py:177
  208.3 31.5 %all_gather.6 = bf16[512,512]{1,0:T(8,128)(2,1)S(1)} all-gather(bf16[64,512]{1,0:T(8,128)(2,1)S(1)} %get-tuple-element.11), channel_id=1, replica_groups=mesh['dp'=8,'chan'=4] {'dp'}, dimensions={0}, use_global_device_ids=true | all-gather | bytes 589824 | tf_op jit(solution)/shard_map/all_gather | solution.py:196
  239.9 0.0 copy-start.3
  239.9 0.0 copy-start.6
  239.9 0.4 fusion.field_ref
  240.3 0.6 copy-done.3
  240.9 0.1 copy-done.6
  241.0 1.7 shard_map.70
  242.7 19.1 %all-reduce.9 = bf16[392,512]{1,0:T(8,128)(2,1)S(1)} all-reduce(f32[392,512]{1,0:T(8,128)S(1)} %get-tuple-element.12), channel_id=1, replica_groups=mesh['dp'=8,'chan'=4] {'chan'}, use_global_device_ids=true, to_apply=%region_3.0 | all-reduce | flops 200704 | bytes 1204224 | tf_op jit(solution)/shard_map/psum | solution.py:190
  261.8 1.4 fusion.12
  263.2 0.0 all-reduce.7.cloned.1.call-update
  263.2 0.2 reduce-scatter.5.cloned.1.call-start
  263.5 1.5 fusion.11
  265.0 0.0 reduce-scatter.5.cloned.1.call-update
  265.0 75.3 %all-reduce.7.cloned.1.call-done.gram_ref = f32[512,512]{1,0:T(8,128)} async-done(((f32[512,512]{1,0:T(8,128)}), f32[512,512]{1,0:T(8,128)}) %all-reduce.7.cloned.1.call-update) | async-done | bytes 1048592 | tf_op jit(solution)/shard_map/psum | solution.py:193
  340.3 66.6 %reduce-scatter.5.cloned.1.call-done.cross_ref = f32[64,512]{1,0:T(8,128)} async-done(((f32[512,512]{1,0:T(8,128)}), f32[64,512]{1,0:T(8,128)}) %reduce-scatter.5.cloned.1.call-update) | async-done | bytes 131088 | tf_op jit(solution)/shard_map/reduce_scatter | solution.py:194
  406.8 0.0 copy-start.1
  406.8 1.2 copy-done.1
  408.1 0.0 copy-start.8
  408.1 0.9 copy-done.8
  409.0 25.1 %shard_map.71 = (bf16[64,512]{1,0:T(8,128)(2,1)S(1)}, f32[512,512]{1,0:T(8,128)S(1)}) custom-call(f32[512,512]{1,0:T(8,128)S(1)} %copy-done.1, f32[64,512]{1,0:T(8,128)S(1)} %copy-done.8), custom_call_target="tpu_custom_call" | custom-call | tf_op jit(solution)/shard_map/pallas_call | solution.py:177
  434.0 31.6 %all_gather.7 = bf16[512,512]{1,0:T(8,128)(2,1)S(1)} all-gather(bf16[64,512]{1,0:T(8,128)(2,1)S(1)} %get-tuple-element.14), channel_id=1, replica_groups=mesh['dp'=8,'chan'=4] {'dp'}, dimensions={0}, use_global_device_ids=true | all-gather | bytes 589824 | tf_op jit(solution)/shard_map/all_gather | solution.py:196
  465.6 1.2 convolution_convert_fusion
  466.7 1.1 broadcast_multiply_fusion
Async XLA Ops:
  7.2 106.3 %all-reduce.5.cloned.1.call-start = ((), (), s32[]{:S(2)}) async-start(), calls=%async_computation.2 | async-start | bytes 2097152 | tf_op jit(solution)/shard_map/psum | solution.py:193
  7.2 1.0 copy-start.2
  8.3 1.0 copy-start.4
  9.3 1.0 copy-start.5
  34.6 145.7 %reduce-scatter.3.cloned.1.call-start = ((), (), s32[]{:S(2)}) async-start(), calls=%async_computation.3 | async-start | bytes 1179648 | tf_op jit(solution)/shard_map/reduce_scatter | solution.py:194
  36.2 304.1 %all-reduce.7.cloned.1.call-start = ((), (), s32[]{:S(2)}) async-start(), calls=%async_computation.4 | async-start | bytes 2097152 | tf_op jit(solution)/shard_map/psum | solution.py:193
  180.3 1.2 copy-start
  181.5 0.9 copy-start.7
  239.9 1.0 copy-start.3
  239.9 1.1 copy-start.6
  263.2 143.6 %reduce-scatter.5.cloned.1.call-start = ((), (), s32[]{:S(2)}) async-start(), calls=%async_computation.5 | async-start | bytes 1179648 | tf_op jit(solution)/shard_map/reduce_scatter | solution.py:194
  406.8 1.2 copy-start.1
  408.1 0.9 copy-start.8
Sparse Core Ops, SparseCore 0:
  34.8 78.6 all-reduce.4
  117.2 63.0 reduce-scatter.2
  263.4 76.8 all-reduce.6
  343.9 62.8 reduce-scatter.4

commit v2 on v1

--- a/solution.py
+++ b/solution.py
@@ -60,7 +60,9 @@
                 full = jnp.where(same, full, jnp.zeros((), BF16))
                 part = dot_bf16(window.astype(BF16), full, ((1,), (0,)))
                 total = part if total is None else total + part
-        out_ref[:, start : start + lanes] = total.astype(BF16)
+        out_ref[0:rows, start : start + lanes] = total.astype(BF16)
+    if out_ref.shape[0] > rows:
+        out_ref[rows:, :] = jnp.zeros((out_ref.shape[0] - rows, width), BF16)
 
 
 def split3(x):
@@ -139,70 +141,203 @@
             big_ref[to, :] = big_ref[to, :] - dot_f32(big_ref[at, to], big_ref[at, :], ((0,), (0,)))
 
 
-def solve_into(gram_ref, cross_ref, mapped_ref, upper_ref, big_ref, work_ref):
-    size = gram_ref.shape[0]
+def identity_into(big_ref, size):
     square = (size, size)
     row_of = lax.broadcasted_iota(jnp.int32, square, 0)
     lane_of = lax.broadcasted_iota(jnp.int32, square, 1)
-    big_ref[:, 0:size] = gram_ref[...]
     big_ref[:, size : 2 * size] = jnp.where(row_of == lane_of, 1.0, 0.0)
+
+
+def exchange(axis, me, count, source, target, send_sem, recv_sem):
+    copies = []
+    for j in range(1, count):
+        peer = lax.rem(me + j, count)
+        copy = pltpu.make_async_remote_copy(
+            src_ref=source(j, peer),
+            dst_ref=target(j, peer),
+            send_sem=send_sem.at[j],
+            recv_sem=recv_sem.at[j],
+            device_id={axis: peer},
+            device_id_type=pl.DeviceIdType.MESH,
+        )
+        copy.start()
+        copies.append(copy)
+    return copies
+
+
+def arrived(axis, me, count, target, send_sem, recv_sem):
+    for j in range(1, count):
+        sender = lax.rem(me + count - j, count)
+        pltpu.make_async_remote_copy(
+            src_ref=target(j, sender),
+            dst_ref=target(j, sender),
+            send_sem=send_sem.at[j],
+            recv_sem=recv_sem.at[j],
+            device_id={axis: sender},
+            device_id_type=pl.DeviceIdType.MESH,
+        ).wait_recv()
+
+
+def layer_kernel(
+    nd, nc, last, total_rows,
+    field_ref, weight_ref, probe_ref, out_ref, upper_ref,
+    pad_ref, resp_ref, part_ref, part_in_ref, sketch_ref, gpart_ref, gin_ref, gsum_ref,
+    cpart_ref, cin_ref, map_ref, big_ref, work_ref,
+    s_part, r_part, s_sketch, r_sketch, s_gram, r_gram, s_rows, r_rows, s_blocks, r_blocks,
+    s_cross, r_cross, s_map, r_map,
+):
+    d = lax.axis_index("dp")
+    c = lax.axis_index("chan")
+    rows, width = field_ref.shape
+    size = probe_ref.shape[1]
+    padded = resp_ref.shape[0]
+    share = size // nc
+    gram_rows = share // nd
+    cross_rows = width // nd
+
+    barrier = pltpu.get_barrier_semaphore()
+    for j in range(1, nd):
+        pl.semaphore_signal(
+            barrier, inc=1, device_id={"dp": lax.rem(d + j, nd)}, device_id_type=pl.DeviceIdType.MESH
+        )
+    for j in range(1, nc):
+        pl.semaphore_signal(
+            barrier, inc=1, device_id={"chan": lax.rem(c + j, nc)}, device_id_type=pl.DeviceIdType.MESH
+        )
+
+    conv_into(field_ref, weight_ref, pad_ref, resp_ref)
+    responses = resp_ref[...]
+    for j in range(nc):
+        block = dot_bf16(responses, probe_ref[:, j * share : (j + 1) * share], ((1,), (0,)))
+        part_ref[j] = block.astype(BF16)
+    pl.semaphore_wait(barrier, nd + nc - 2)
+
+    started = exchange(
+        "chan", c, nc, lambda j, p: part_ref.at[p], lambda j, p: part_in_ref.at[j], s_part, r_part
+    )
+    identity_into(big_ref, size)
+    arrived("chan", c, nc, lambda j, p: part_in_ref.at[j], s_part, r_part)
+    mine = part_ref[c].astype(F32)
+    for j in range(1, nc):
+        mine = mine + part_in_ref[j].astype(F32)
+    mine = mine.astype(BF16)
+    sketch_ref[c] = mine
+    started += exchange(
+        "chan", c, nc, lambda j, p: sketch_ref.at[c], lambda j, p: sketch_ref.at[c], s_sketch, r_sketch
+    )
+    arrived("chan", c, nc, lambda j, p: sketch_ref.at[p], s_sketch, r_sketch)
+    sketch = jnp.concatenate([sketch_ref[j] for j in range(nc)], axis=1)
+
+    gram = dot_bf16(mine, sketch, ((0,), (0,)))
+    for j in range(nd):
+        gpart_ref[j] = gram[j * gram_rows : (j + 1) * gram_rows, :]
+    started += exchange(
+        "dp", d, nd, lambda j, p: gpart_ref.at[p], lambda j, p: gin_ref.at[j], s_gram, r_gram
+    )
+    cross = dot_bf16(responses, sketch, ((0,), (0,)))
+    for j in range(nd):
+        cpart_ref[j] = cross[j * cross_rows : (j + 1) * cross_rows, :]
+    arrived("dp", d, nd, lambda j, p: gin_ref.at[j], s_gram, r_gram)
+    total = gpart_ref[d]
+    for j in range(1, nd):
+        total = total + gin_ref[j]
+    gsum_ref[c, d] = total
+    started += exchange(
+        "dp", d, nd, lambda j, p: gsum_ref.at[c, d], lambda j, p: gsum_ref.at[c, d], s_rows, r_rows
+    )
+    arrived("dp", d, nd, lambda j, p: gsum_ref.at[c, p], s_rows, r_rows)
+    started += exchange(
+        "chan", c, nc, lambda j, p: gsum_ref.at[c], lambda j, p: gsum_ref.at[c], s_blocks, r_blocks
+    )
+    arrived("chan", c, nc, lambda j, p: gsum_ref.at[p], s_blocks, r_blocks)
+    started += exchange(
+        "dp", d, nd, lambda j, p: cpart_ref.at[p], lambda j, p: cin_ref.at[j], s_cross, r_cross
+    )
+    for k in range(nc):
+        for j in range(nd):
+            top = k * share + j * gram_rows
+            big_ref[top : top + gram_rows, 0:size] = gsum_ref[k, j]
+
     eliminate(big_ref, work_ref, size)
-    if upper_ref is not None:
-        upper_ref[...] = jnp.where(lane_of >= row_of, big_ref[:, 0:size], 0.0)
+    if last:
+        square = (size, size)
+        keep = lax.broadcasted_iota(jnp.int32, square, 1) >= lax.broadcasted_iota(jnp.int32, square, 0)
+        upper_ref[...] = jnp.where(keep, big_ref[:, 0:size], 0.0) * (1.0 / math.sqrt(total_rows))
+
+    arrived("dp", d, nd, lambda j, p: cin_ref.at[j], s_cross, r_cross)
+    own = cpart_ref[d]
+    for j in range(1, nd):
+        own = own + cin_ref[j]
     inverse = big_ref[:, size : 2 * size]
-    coeffs = dot_f32(cross_ref[...], inverse, ((1,), (1,))).astype(BF16)
-    mapped_ref[...] = dot_f32(coeffs.astype(F32), inverse, ((1,), (0,))).astype(BF16)
-
-
-def conv_kernel(field_ref, weight_ref, probe_ref, responses_ref, partial_ref, pad_ref):
-    conv_into(field_ref, weight_ref, pad_ref, responses_ref)
-    partial_ref[...] = dot_bf16(responses_ref[...], probe_ref[...], ((1,), (0,)))
-
-
-def conv_call(field, weight, probe):
+    coeffs = dot_f32(own, inverse, ((1,), (1,))).astype(BF16)
+    map_ref[d] = dot_f32(coeffs.astype(F32), inverse, ((1,), (0,))).astype(BF16)
+    started += exchange(
+        "dp", d, nd, lambda j, p: map_ref.at[d], lambda j, p: map_ref.at[d], s_map, r_map
+    )
+    arrived("dp", d, nd, lambda j, p: map_ref.at[p], s_map, r_map)
+    if cross_rows % 16 == 0:
+        mapped = jnp.concatenate([map_ref[j] for j in range(nd)], axis=0)
+    else:
+        mapped = jnp.concatenate([map_ref[j].astype(F32) for j in range(nd)], axis=0).astype(BF16)
+    restored = dot_bf16(sketch, mapped, ((1,), (1,)))
+    if not last:
+        restored = jnp.maximum(restored, 0.0)
+    out_ref[...] = restored[0:rows, :].astype(BF16)
+    for copy in started:
+        copy.wait_send()
+
+
+def first_kernel(nd, nc, total_rows, field_ref, weight_ref, probe_ref, out_ref, *rest):
+    layer_kernel(nd, nc, False, total_rows, field_ref, weight_ref, probe_ref, out_ref, None, *rest)
+
+
+def last_kernel(nd, nc, total_rows, *refs):
+    layer_kernel(nd, nc, True, total_rows, *refs)
+
+
+def layer(field, weight, probe, last):
+    nd, nc = lax.axis_size("dp"), lax.axis_size("chan")
     rows, width = field.shape
+    size = probe.shape[1]
+    padded = -(-rows // 16) * 16
+    share = size // nc
+    gram_rows = share // nd
+    cross_rows = width // nd
+    restored = jax.ShapeDtypeStruct((rows, width), BF16)
+    upper = jax.ShapeDtypeStruct((size, size), F32)
+    chan_sems = pltpu.SemaphoreType.DMA((nc,))
+    dp_sems = pltpu.SemaphoreType.DMA((nd,))
     return pl.pallas_call(
-        conv_kernel,
-        out_shape=(
-            jax.ShapeDtypeStruct((rows, width), BF16),
-            jax.ShapeDtypeStruct((rows, probe.shape[1]), F32),
+        functools.partial(last_kernel if last else first_kernel, nd, nc, rows * nd),
+        out_shape=(restored, upper) if last else restored,
+        scratch_shapes=[
+            pltpu.VMEM((rows + 2 * PAD, width), F32),
+            pltpu.VMEM((padded, width), BF16),
+            pltpu.VMEM((nc, padded, share), BF16),
+            pltpu.VMEM((nc, padded, share), BF16),
+            pltpu.VMEM((nc, padded, share), BF16),
+            pltpu.VMEM((nd, gram_rows, size), F32),
+            pltpu.VMEM((nd, gram_rows, size), F32),
+            pltpu.VMEM((nc, nd, gram_rows, size), F32),
+            pltpu.VMEM((nd, cross_rows, size), F32),
+            pltpu.VMEM((nd, cross_rows, size), F32),
+            pltpu.VMEM((nd, cross_rows, size), BF16),
+            pltpu.VMEM((size, 2 * size), F32),
+            pltpu.VMEM((BLOCK, 2 * BLOCK), F32),
+        ]
+        + [chan_sems] * 4
+        + [dp_sems] * 4
+        + [chan_sems] * 2
+        + [dp_sems] * 4,
+        compiler_params=pltpu.CompilerParams(
+            vmem_limit_bytes=VMEM_LIMIT, collective_id=1 if last else 0, has_side_effects=True
         ),
-        scratch_shapes=[pltpu.VMEM((rows + 2 * PAD, width), F32)],
-        compiler_params=pltpu.CompilerParams(vmem_limit_bytes=VMEM_LIMIT),
     )(field, weight, probe)
 
 
-def solve_call(gram, cross):
-    size = gram.shape[0]
-    return pl.pallas_call(
-        solve_into,
-        out_shape=(
-            jax.ShapeDtypeStruct(cross.shape, BF16),
-            jax.ShapeDtypeStruct(gram.shape, F32),
-        ),
-        scratch_shapes=[pltpu.VMEM((size, 2 * size), F32), pltpu.VMEM((BLOCK, 2 * BLOCK), F32)],
-        compiler_params=pltpu.CompilerParams(vmem_limit_bytes=VMEM_LIMIT),
-    )(gram, cross)
-
-
-def layer(field, weight, probe):
-    responses, partial = conv_call(field, weight, probe)
-    sketch = lax.psum(partial, "chan").astype(BF16)
-    gram = dot_bf16(sketch, sketch, ((0,), (0,)))
-    cross = dot_bf16(responses, sketch, ((0,), (0,)))
-    gram = lax.psum(gram, "dp")
-    cross = lax.psum_scatter(cross, "dp", scatter_dimension=0, tiled=True)
-    mapped, upper = solve_call(gram, cross)
-    mapped = lax.all_gather(mapped, "dp", axis=0, tiled=True)
-    return dot_bf16(sketch, mapped, ((1,), (1,))).astype(BF16), upper
-
-
 def per_device(inputs, conv_one, conv_two, probe_one, probe_two):
-    restored_one, _ = layer(inputs, conv_one, probe_one)
-    activated = jnp.maximum(restored_one, jnp.zeros((), BF16))
-    restored, upper = layer(activated, conv_two, probe_two)
-    total_rows = inputs.shape[0] * lax.axis_size("dp")
-    return (restored, upper * (1.0 / math.sqrt(total_rows)))
+    activated = layer(inputs, conv_one, probe_one, False)
+    return layer(activated, conv_two, probe_two, True)
 
 
 def solution(mesh):

time: 475 us -> 157 us (0.33)
  the two profiles are of different devices: /device:TPU:0 before, /device:TPU:15 now
where the time goes in v2:
time: 157 us
  Pallas kernels  152 us (97%)
  local copies, waits for them, and re-layouts  4.72 us (3%)
    pallas_call x2, Pallas kernels, layer(): pl.pallas_call(functools.partial(last_kernel if last else first_kernel, n...  152 us
    unnamed x12, local copies, waits for them, and re-layouts  4.72 us

profile of v2, /device:TPU:15, one launch (start us, length us, event | category | flops | bytes accessed | tf_op | source)
XLA Modules:
  0.0 156.9 jit_solution(17875160075953009506)
XLA Ops:
  0.6 0.0 copy-start
  0.6 1.0 copy-done
  1.7 0.0 copy-start.2
  1.7 1.0 copy-done.2
  2.7 0.0 copy-start.3
  2.7 1.0 copy-done.3
  3.6 0.0 copy-start.1
  3.6 0.0 copy-start.4
  3.6 75.1 %shard_map.68.refs_0_ = bf16[392,512]{1,0:T(8,128)(2,1)S(1)} custom-call(bf16[392,512]{1,0:T(8,128)(2,1)S(1)} %copy-done.2, bf16[9,32,512]{2,1,0:T(8,128)(2,1)S(1)} %copy-done.3, bf16[512,512]{1,0:T(8,128)(2,1)S(1)} %copy-done), custom_call_target="tpu_custom_call" | custom-call | tf_op jit(solution)/shard_map/pallas_call | solution.py:310
  78.8 0.0 copy-done.1
  78.8 0.0 copy-done.4
  78.8 76.4 %shard_map.69 = (bf16[392,512]{1,0:T(8,128)(2,1)S(1)}, f32[512,512]{1,0:T(8,128)S(1)}) custom-call(bf16[392,512]{1,0:T(8,128)(2,1)S(1)} %shard_map.68.refs_0_, bf16[9,32,512]{2,1,0:T(8,128)(2,1)S(1)} %copy-done.4, bf16[512,512]{1,0:T(8,128)(2,1)S(1)} %copy-done.1), custom_call_target="tpu_custom_call" | custom-call | tf_op jit(solution)/shard_map/pallas_call | solution.py:310
  155.2 0.8 copy.9
  155.9 1.0 copy.10
Async XLA Ops:
  0.6 1.0 copy-start
  1.7 1.0 copy-start.2
  2.7 1.0 copy-start.3
  3.6 75.1 %copy-start.1 = (bf16[512,512]{1,0:T(8,128)(2,1)S(1)}, bf16[512,512]{1,0:T(8,128)(2,1)}, u32[]{:S(2)}) copy-start(bf16[512,512]{1,0:T(8,128)(2,1)} %refs_2_.1) | copy-start | bytes 1572868
  3.6 75.2 %copy-start.4 = (bf16[9,32,512]{2,1,0:T(8,128)(2,1)S(1)}, bf16[9,32,512]{2,1,0:T(8,128)(2,1)}, u32[]{:S(2)}) copy-start(bf16[9,32,512]{2,1,0:T(8,128)(2,1)} %refs_1_.1) | copy-start | bytes 884740

commit v3 on v2

--- a/solution.py
+++ b/solution.py
@@ -71,6 +71,16 @@
     middle = rest.astype(BF16)
     low = (rest - middle.astype(F32)).astype(BF16)
     return high, middle, low
+
+
+def stack_first(x, axis):
+    h, m, l = split3(x)
+    return jnp.concatenate([h, h, m, h, l, m], axis=axis)
+
+
+def stack_second(x):
+    h, m, l = split3(x)
+    return jnp.concatenate([h, m, h, l, h, m], axis=0)
 
 
 def eliminate_block(work_ref):
@@ -102,21 +112,12 @@
         work_ref[top : top + PANEL, BLOCK : 2 * BLOCK] = right
         if top + PANEL < BLOCK:
             rest = top + PANEL
-            h, m, l = split3(left)
-            hr, mr, lr = split3(right)
-            first = jnp.concatenate([h, h, m, h, l, m], axis=0)
-            second = jnp.concatenate(
-                [
-                    jnp.concatenate([h, m, h, l, h, m], axis=0),
-                    jnp.concatenate([hr, mr, hr, lr, hr, mr], axis=0),
-                ],
-                axis=1,
-            )
-            update = dot_bf16(first, second, ((0,), (0,)))
+            second = jnp.concatenate([stack_second(left), stack_second(right)], axis=1)
+            update = dot_bf16(stack_first(left, 0), second, ((0,), (0,)))
             work_ref[rest:BLOCK, :] = work_ref[rest:BLOCK, :] - update[rest:BLOCK, :]
 
 
-def eliminate(big_ref, work_ref, size):
+def eliminate(big_ref, work_ref, stack_ref, diag_ref, size, between):
     blocks = size // BLOCK
     square = (BLOCK, BLOCK)
     eye = jnp.where(
@@ -127,25 +128,24 @@
 
     @pl.loop(0, blocks)
     def _(b):
+        pl.when(b == 1)(between)
         at = pl.ds(pl.multiple_of(b * BLOCK, BLOCK), BLOCK)
         work_ref[:, 0:BLOCK] = big_ref[at, at]
         work_ref[:, BLOCK : 2 * BLOCK] = eye
         eliminate_block(work_ref)
+        diag_ref[b] = work_ref[:, 0:BLOCK]
         inverse = work_ref[:, BLOCK : 2 * BLOCK]
-        big_ref[at, :] = dot_f32(inverse, big_ref[at, :], ((1,), (0,)))
-        big_ref[at, at] = work_ref[:, 0:BLOCK]
+        big_ref[at, at] = eye
+        row = dot_bf16(stack_first(inverse, 1), stack_second(big_ref[at, :]), ((1,), (0,)))
+        big_ref[at, :] = row
+        stack_ref[...] = stack_second(row)
 
         @pl.loop(b + 1, blocks)
         def _(other):
             to = pl.ds(pl.multiple_of(other * BLOCK, BLOCK), BLOCK)
-            big_ref[to, :] = big_ref[to, :] - dot_f32(big_ref[at, to], big_ref[at, :], ((0,), (0,)))
-
-
-def identity_into(big_ref, size):
-    square = (size, size)
-    row_of = lax.broadcasted_iota(jnp.int32, square, 0)
-    lane_of = lax.broadcasted_iota(jnp.int32, square, 1)
-    big_ref[:, size : 2 * size] = jnp.where(row_of == lane_of, 1.0, 0.0)
+            big_ref[to, at] = jnp.zeros(square, F32)
+            factor = stack_first(big_ref[at, to], 0)
+            big_ref[to, :] = big_ref[to, :] - dot_bf16(factor, stack_ref[...], ((0,), (0,)))
 
 
 def exchange(axis, me, count, source, target, send_sem, recv_sem):
@@ -178,13 +178,58 @@
         ).wait_recv()
 
 
+def send(axis, peer, source, target, send_sem, recv_sem):
+    copy = pltpu.make_async_remote_copy(
+        src_ref=source,
+        dst_ref=target,
+        send_sem=send_sem,
+        recv_sem=recv_sem,
+        device_id={axis: peer},
+        device_id_type=pl.DeviceIdType.MESH,
+    )
+    copy.start()
+    return copy
+
+
+def expect(axis, sender, target, send_sem, recv_sem):
+    pltpu.make_async_remote_copy(
+        src_ref=target,
+        dst_ref=target,
+        send_sem=send_sem,
+        recv_sem=recv_sem,
+        device_id={axis: sender},
+        device_id_type=pl.DeviceIdType.MESH,
+    ).wait_recv()
+
+
+def gather(axis, me, count, slot, far_send, far_recv, mate_send, mate_recv):
+    high, low = me // 2, me % 2
+    mate = me + 1 - 2 * low
+    pairs = count // 2
+    copies = [
+        send(axis, 2 * lax.rem(high + j, pairs) + low, slot(me), slot(me), far_send.at[j], far_recv.at[j])
+        for j in range(1, pairs)
+    ]
+    copies.append(send(axis, mate, slot(me), slot(me), mate_send.at[0], mate_recv.at[0]))
+    for j in range(1, pairs):
+        sender = 2 * lax.rem(high + pairs - j, pairs) + low
+        expect(axis, sender, slot(sender), far_send.at[j], far_recv.at[j])
+        copies.append(send(axis, mate, slot(sender), slot(sender), mate_send.at[j], mate_recv.at[j]))
+    expect(axis, mate, slot(mate), mate_send.at[0], mate_recv.at[0])
+    for j in range(1, pairs):
+        origin = 2 * lax.rem(high + pairs - j, pairs) + 1 - low
+        expect(axis, mate, slot(origin), mate_send.at[j], mate_recv.at[j])
+    return copies
+
+
 def layer_kernel(
     nd, nc, last, total_rows,
     field_ref, weight_ref, probe_ref, out_ref, upper_ref,
     pad_ref, resp_ref, part_ref, part_in_ref, sketch_ref, gpart_ref, gin_ref, gsum_ref,
-    cpart_ref, cin_ref, map_ref, big_ref, work_ref,
-    s_part, r_part, s_sketch, r_sketch, s_gram, r_gram, s_rows, r_rows, s_blocks, r_blocks,
-    s_cross, r_cross, s_map, r_map,
+    cpart_ref, cmate_ref, cin_ref, map_ref, big_ref, work_ref, stack_ref, diag_ref,
+    s_part, r_part, s_sketch, r_sketch, s_sketch2, r_sketch2, s_blocks, r_blocks, s_blocks2, r_blocks2,
+    s_gram, r_gram, s_rows, r_rows, s_rows2, r_rows2, s_mate, r_mate, s_cross, r_cross,
+    s_map, r_map, s_map2, r_map2,
 ):
     d = lax.axis_index("dp")
     c = lax.axis_index("chan")
@@ -215,66 +260,110 @@
     started = exchange(
         "chan", c, nc, lambda j, p: part_ref.at[p], lambda j, p: part_in_ref.at[j], s_part, r_part
     )
-    identity_into(big_ref, size)
+    big_ref[...] = jnp.zeros((size, size), F32)
     arrived("chan", c, nc, lambda j, p: part_in_ref.at[j], s_part, r_part)
     mine = part_ref[c].astype(F32)
     for j in range(1, nc):
         mine = mine + part_in_ref[j].astype(F32)
     mine = mine.astype(BF16)
     sketch_ref[c] = mine
-    started += exchange(
-        "chan", c, nc, lambda j, p: sketch_ref.at[c], lambda j, p: sketch_ref.at[c], s_sketch, r_sketch
-    )
-    arrived("chan", c, nc, lambda j, p: sketch_ref.at[p], s_sketch, r_sketch)
+    started += gather(
+        "chan", c, nc, lambda i: sketch_ref.at[i], s_sketch, r_sketch, s_sketch2, r_sketch2
+    )
     sketch = jnp.concatenate([sketch_ref[j] for j in range(nc)], axis=1)
 
-    gram = dot_bf16(mine, sketch, ((0,), (0,)))
+    half = nc // 2
+    ahead = [mine] + [sketch_ref[lax.rem(c + k, nc)] for k in range(1, half + 1)]
+    gram = dot_bf16(mine, jnp.concatenate(ahead, axis=1), ((0,), (0,)))
     for j in range(nd):
         gpart_ref[j] = gram[j * gram_rows : (j + 1) * gram_rows, :]
     started += exchange(
         "dp", d, nd, lambda j, p: gpart_ref.at[p], lambda j, p: gin_ref.at[j], s_gram, r_gram
     )
+    pairs = nd // 2
+    high, low = d // 2, d % 2
+    mate = d + 1 - 2 * low
     cross = dot_bf16(responses, sketch, ((0,), (0,)))
     for j in range(nd):
-        cpart_ref[j] = cross[j * cross_rows : (j + 1) * cross_rows, :]
+        cpart_ref[j % 2, j // 2] = cross[j * cross_rows : (j + 1) * cross_rows, :]
     arrived("dp", d, nd, lambda j, p: gin_ref.at[j], s_gram, r_gram)
     total = gpart_ref[d]
     for j in range(1, nd):
         total = total + gin_ref[j]
     gsum_ref[c, d] = total
-    started += exchange(
-        "dp", d, nd, lambda j, p: gsum_ref.at[c, d], lambda j, p: gsum_ref.at[c, d], s_rows, r_rows
-    )
-    arrived("dp", d, nd, lambda j, p: gsum_ref.at[c, p], s_rows, r_rows)
-    started += exchange(
-        "chan", c, nc, lambda j, p: gsum_ref.at[c], lambda j, p: gsum_ref.at[c], s_blocks, r_blocks
-    )
-    arrived("chan", c, nc, lambda j, p: gsum_ref.at[p], s_blocks, r_blocks)
-    started += exchange(
-        "dp", d, nd, lambda j, p: cpart_ref.at[p], lambda j, p: cin_ref.at[j], s_cross, r_cross
-    )
-    for k in range(nc):
-        for j in range(nd):
-            top = k * share + j * gram_rows
-            big_ref[top : top + gram_rows, 0:size] = gsum_ref[k, j]
-
-    eliminate(big_ref, work_ref, size)
+    started += gather("dp", d, nd, lambda i: gsum_ref.at[c, i], s_rows, r_rows, s_rows2, r_rows2)
+    started.append(
+        send("dp", mate, cpart_ref.at[1 - low], cmate_ref, s_mate.at[0], r_mate.at[0])
+    )
+    started += gather(
+        "chan", c, nc, lambda i: gsum_ref.at[i], s_blocks, r_blocks, s_blocks2, r_blocks2
+    )
+    for first in range(nc):
+        for k in range(half + 1):
+            second = first + k
+            lanes = slice(k * share, (k + 1) * share)
+            if second < nc:
+                for j in range(nd):
+                    top = first * share + j * gram_rows
+                    big_ref[top : top + gram_rows, second * share : (second + 1) * share] = gsum_ref[
+                        first, j, :, lanes
+                    ]
+            elif k < half:
+                for j in range(nd):
+                    work_ref[j * gram_rows : (j + 1) * gram_rows, 0:share] = gsum_ref[first, j, :, lanes]
+                second -= nc
+                big_ref[
+                    second * share : (second + 1) * share, first * share : (first + 1) * share
+                ] = jnp.transpose(work_ref[0:share, 0:share])
+    if share < BLOCK:
+        full = big_ref[...]
+        square = (size, size)
+        above = lax.broadcasted_iota(jnp.int32, square, 1) > lax.broadcasted_iota(jnp.int32, square, 0)
+        big_ref[...] = jnp.where(above, full, jnp.transpose(full))
+
+    def between():
+        expect("dp", mate, cmate_ref, s_mate.at[0], r_mate.at[0])
+        cmate_ref[...] = cmate_ref[...] + cpart_ref[low]
+        for j in range(1, pairs):
+            place = lax.rem(high + j, pairs)
+            send("dp", 2 * place + low, cmate_ref.at[place], cin_ref.at[j], s_cross.at[j], r_cross.at[j])
+
+    eliminate(big_ref, work_ref, stack_ref, diag_ref, size, between)
+    square = (size, size)
+    row_of = lax.broadcasted_iota(jnp.int32, square, 0)
+    lane_of = lax.broadcasted_iota(jnp.int32, square, 1)
+    inverse = jnp.where(lane_of <= row_of, big_ref[...], 0.0)
+    ih, im, il = split3(inverse)
+    own = cmate_ref[high]
+    for j in range(1, pairs):
+        sender = 2 * lax.rem(high + pairs - j, pairs) + low
+        expect("dp", sender, cin_ref.at[j], s_cross.at[j], r_cross.at[j])
+        own = own + cin_ref[j]
+    oh, om, ol = split3(own)
+    inner = ((1,), (1,))
+    coeffs = dot_bf16(oh, il, inner) + dot_bf16(om, im, inner) + dot_bf16(ol, ih, inner)
+    coeffs = coeffs + dot_bf16(oh, im, inner) + dot_bf16(om, ih, inner)
+    coeffs = (coeffs + dot_bf16(oh, ih, inner)).astype(BF16)
+    outer = ((1,), (0,))
+    mapped = dot_bf16(coeffs, il, outer) + dot_bf16(coeffs, im, outer)
+    map_ref[d] = (mapped + dot_bf16(coeffs, ih, outer)).astype(BF16)
+    started += gather("dp", d, nd, lambda i: map_ref.at[i], s_map, r_map, s_map2, r_map2)
     if last:
-        square = (size, size)
-        keep = lax.broadcasted_iota(jnp.int32, square, 1) >= lax.broadcasted_iota(jnp.int32, square, 0)
-        upper_ref[...] = jnp.where(keep, big_ref[:, 0:size], 0.0) * (1.0 / math.sqrt(total_rows))
-
-    arrived("dp", d, nd, lambda j, p: cin_ref.at[j], s_cross, r_cross)
-    own = cpart_ref[d]
-    for j in range(1, nd):
-        own = own + cin_ref[j]
-    inverse = big_ref[:, size : 2 * size]
-    coeffs = dot_f32(own, inverse, ((1,), (1,))).astype(BF16)
-    map_ref[d] = dot_f32(coeffs.astype(F32), inverse, ((1,), (0,))).astype(BF16)
-    started += exchange(
-        "dp", d, nd, lambda j, p: map_ref.at[d], lambda j, p: map_ref.at[d], s_map, r_map
-    )
-    arrived("dp", d, nd, lambda j, p: map_ref.at[p], s_map, r_map)
+        scale = 1.0 / math.sqrt(total_rows)
+        upper_ref[...] = jnp.where(lane_of >= row_of, big_ref[...], 0.0) * scale
+        for b in range(size // BLOCK):
+            at = slice(b * BLOCK, (b + 1) * BLOCK)
+            upper_ref[at, at] = diag_ref[b] * scale
+    for j in range(1, pairs):
+        place = lax.rem(high + j, pairs)
+        pltpu.make_async_remote_copy(
+            src_ref=cmate_ref.at[place],
+            dst_ref=cin_ref.at[j],
+            send_sem=s_cross.at[j],
+            recv_sem=r_cross.at[j],
+            device_id={"dp": 2 * place + low},
+            device_id_type=pl.DeviceIdType.MESH,
+        ).wait_send()
     if cross_rows % 16 == 0:
         mapped = jnp.concatenate([map_ref[j] for j in range(nd)], axis=0)
     else:
@@ -302,6 +391,7 @@
     padded = -(-rows // 16) * 16
     share = size // nc
     gram_rows = share // nd
+    gram_lanes = (nc // 2 + 1) * share
     cross_rows = width // nd
     restored = jax.ShapeDtypeStruct((rows, width), BF16)
     upper = jax.ShapeDtypeStruct((size, size), F32)
@@ -316,19 +406,20 @@
             pltpu.VMEM((nc, padded, share), BF16),
             pltpu.VMEM((nc, padded, share), BF16),
             pltpu.VMEM((nc, padded, share), BF16),
-            pltpu.VMEM((nd, gram_rows, size), F32),
-            pltpu.VMEM((nd, gram_rows, size), F32),
-            pltpu.VMEM((nc, nd, gram_rows, size), F32),
-            pltpu.VMEM((nd, cross_rows, size), F32),
-            pltpu.VMEM((nd, cross_rows, size), F32),
+            pltpu.VMEM((nd, gram_rows, gram_lanes), F32),
+            pltpu.VMEM((nd, gram_rows, gram_lanes), F32),
+            pltpu.VMEM((nc, nd, gram_rows, gram_lanes), F32),
+            pltpu.VMEM((2, nd // 2, cross_rows, size), F32),
+            pltpu.VMEM((nd // 2, cross_rows, size), F32),
+            pltpu.VMEM((nd // 2, cross_rows, size), F32),
             pltpu.VMEM((nd, cross_rows, size), BF16),
-            pltpu.VMEM((size, 2 * size), F32),
+            pltpu.VMEM((size, size), F32),
             pltpu.VMEM((BLOCK, 2 * BLOCK), F32),
+            pltpu.VMEM((6 * BLOCK, size), BF16),
+            pltpu.VMEM((size // BLOCK, BLOCK, BLOCK), F32),
         ]
-        + [chan_sems] * 4
-        + [dp_sems] * 4
-        + [chan_sems] * 2
-        + [dp_sems] * 4,
+        + [chan_sems] * 10
+        + [dp_sems] * 14,
         compiler_params=pltpu.CompilerParams(
             vmem_limit_bytes=VMEM_LIMIT, collective_id=1 if last else 0, has_side_effects=True
         ),

time: 157 us -> 145 us (0.924)
  the two profiles are of different devices: /device:TPU:15 before, /device:TPU:0 now
where the time goes in v3:
time: 145 us
  Pallas kernels  139 us (96%)
  local copies, waits for them, and re-layouts  4.72 us (3%)
    pallas_call x2, Pallas kernels, layer(): pl.pallas_call(functools.partial(last_kernel if last else first_kernel, n...  139 us
    unnamed x12, local copies, waits for them, and re-layouts  4.72 us

profile of v3, /device:TPU:0, one launch (start us, length us, event | category | flops | bytes accessed | tf_op | source)
XLA Modules:
  0.0 144.5 jit_solution(13599849791053415091)
XLA Ops:
  0.6 0.0 copy-start
  0.6 1.0 copy-done
  1.7 0.0 copy-start.2
  1.7 1.0 copy-done.2
  2.7 0.0 copy-start.3
  2.7 1.0 copy-done.3
  3.6 0.0 copy-start.1
  3.6 0.0 copy-start.4
  3.6 70.7 %shard_map.68.refs_0_ = bf16[392,512]{1,0:T(8,128)(2,1)S(1)} custom-call(bf16[392,512]{1,0:T(8,128)(2,1)S(1)} %copy-done.2, bf16[9,32,512]{2,1,0:T(8,128)(2,1)S(1)} %copy-done.3, bf16[512,512]{1,0:T(8,128)(2,1)S(1)} %copy-done), custom_call_target="tpu_custom_call" | custom-call | tf_op jit(solution)/shard_map/pallas_call | solution.py:400
  74.4 0.0 copy-done.1
  74.4 0.0 copy-done.4
  74.4 68.4 %shard_map.69 = (bf16[392,512]{1,0:T(8,128)(2,1)S(1)}, f32[512,512]{1,0:T(8,128)S(1)}) custom-call(bf16[392,512]{1,0:T(8,128)(2,1)S(1)} %shard_map.68.refs_0_, bf16[9,32,512]{2,1,0:T(8,128)(2,1)S(1)} %copy-done.4, bf16[512,512]{1,0:T(8,128)(2,1)S(1)} %copy-done.1), custom_call_target="tpu_custom_call" | custom-call | tf_op jit(solution)/shard_map/pallas_call | solution.py:400
  142.8 0.8 copy.9
  143.5 1.0 copy.10
Async XLA Ops:
  0.6 1.0 copy-start
  1.7 1.0 copy-start.2
  2.7 1.0 copy-start.3
  3.6 70.7 %copy-start.1 = (bf16[512,512]{1,0:T(8,128)(2,1)S(1)}, bf16[512,512]{1,0:T(8,128)(2,1)}, u32[]{:S(2)}) copy-start(bf16[512,512]{1,0:T(8,128)(2,1)} %refs_2_.1) | copy-start | bytes 1572868
  3.6 70.7 %copy-start.4 = (bf16[9,32,512]{2,1,0:T(8,128)(2,1)S(1)}, bf16[9,32,512]{2,1,0:T(8,128)(2,1)}, u32[]{:S(2)}) copy-start(bf16[9,32,512]{2,1,0:T(8,128)(2,1)} %refs_1_.1) | copy-start | bytes 884740

commit v4 on v3

--- a/solution.py
+++ b/solution.py
@@ -96,11 +96,14 @@
         for i in range(PANEL):
             pivot = jnp.broadcast_to(cols[i][i : i + 1, :], (PANEL, BLOCK))
             root = lax.rsqrt(pivot)
-            root = root * (1.5 - 0.5 * pivot * root * root)
             scale = jnp.where(row_of == i, root, scale)
             if i < PANEL - 1:
-                factor = jnp.where(row_of > i, cols[i] * (root * root), 0.0)
-                for k in range(i + 1, PANEL):
+                below = jnp.where(row_of > i, cols[i], 0.0)
+                ahead = below * cols[i + 1][i : i + 1, :]
+                square = root * root
+                cols[i + 1] = cols[i + 1] - ahead * square
+                factor = below * square
+                for k in range(i + 2, PANEL):
                     cols[k] = cols[k] - factor * cols[k][i : i + 1, :]
                 left = left - factor * left[i : i + 1, :]
                 right = right - factor * right[i : i + 1, :]
@@ -128,7 +131,8 @@
 
     @pl.loop(0, blocks)
     def _(b):
-        pl.when(b == 1)(between)
+        for step, task in enumerate(between):
+            pl.when(b == step + 1)(task)
         at = pl.ds(pl.multiple_of(b * BLOCK, BLOCK), BLOCK)
         work_ref[:, 0:BLOCK] = big_ref[at, at]
         work_ref[:, BLOCK : 2 * BLOCK] = eye
@@ -222,15 +226,78 @@
     return copies
 
 
+def gather_rows(d, nd, c, nc, slot, far, mate_sems, chan_far, chan_mate, middle):
+    high, low = d // 2, d % 2
+    mate = d + 1 - 2 * low
+    pairs = nd // 2
+    chan_high, chan_low = c // 2, c % 2
+    chan_other = c + 1 - 2 * chan_low
+    chan_pairs = nc // 2
+    copies = []
+
+    def over_chan(order, piece):
+        ref = slot(c, piece)
+        for j in range(1, chan_pairs):
+            peer = 2 * lax.rem(chan_high + j, chan_pairs) + chan_low
+            copies.append(send("chan", peer, ref, ref, chan_far[0].at[order, j], chan_far[1].at[order, j]))
+        copies.append(send("chan", chan_other, ref, ref, chan_mate[0].at[order, 0], chan_mate[1].at[order, 0]))
+
+    mine = slot(c, d)
+    for j in range(1, pairs):
+        peer = 2 * lax.rem(high + j, pairs) + low
+        copies.append(send("dp", peer, mine, mine, far[0].at[j], far[1].at[j]))
+    copies.append(send("dp", mate, mine, mine, mate_sems[0].at[0], mate_sems[1].at[0]))
+    over_chan(0, d)
+    pieces = [d, mate]
+    expect("dp", mate, slot(c, mate), mate_sems[0].at[0], mate_sems[1].at[0])
+    over_chan(1, mate)
+    for j in range(1, pairs):
+        sender = 2 * lax.rem(high + pairs - j, pairs) + low
+        piece = slot(c, sender)
+        expect("dp", sender, piece, far[0].at[j], far[1].at[j])
+        copies.append(send("dp", mate, piece, piece, mate_sems[0].at[j], mate_sems[1].at[j]))
+        over_chan(2 * j, sender)
+        pieces.append(sender)
+        origin = 2 * lax.rem(high + pairs - j, pairs) + 1 - low
+        expect("dp", mate, slot(c, origin), mate_sems[0].at[j], mate_sems[1].at[j])
+        over_chan(2 * j + 1, origin)
+        pieces.append(origin)
+    middle()
+    for order, piece in enumerate(pieces):
+        for j in range(1, chan_pairs):
+            sender = 2 * lax.rem(chan_high + chan_pairs - j, chan_pairs) + chan_low
+            ref = slot(sender, piece)
+            expect("chan", sender, ref, chan_far[0].at[order, j], chan_far[1].at[order, j])
+            copies.append(
+                send("chan", chan_other, ref, ref, chan_mate[0].at[order, j], chan_mate[1].at[order, j])
+            )
+    for order, piece in enumerate(pieces):
+        for j in range(chan_pairs):
+            origin = 2 * lax.rem(chan_high + chan_pairs - j, chan_pairs) + 1 - chan_low
+            expect(
+                "chan", chan_other, slot(origin, piece), chan_mate[0].at[order, j], chan_mate[1].at[order, j]
+            )
+    return copies
+
+
 def layer_kernel(
     nd, nc, last, total_rows,
-    field_ref, weight_ref, probe_ref, out_ref, upper_ref,
+    field_any, weight_any, probe_any, out_ref, upper_ref,
     pad_ref, resp_ref, part_ref, part_in_ref, sketch_ref, gpart_ref, gin_ref, gsum_ref,
     cpart_ref, cmate_ref, cin_ref, map_ref, big_ref, work_ref, stack_ref, diag_ref,
-    s_part, r_part, s_sketch, r_sketch, s_sketch2, r_sketch2, s_blocks, r_blocks, s_blocks2, r_blocks2,
+    s_part, r_part, s_sketch, r_sketch, s_sketch2, r_sketch2,
     s_gram, r_gram, s_rows, r_rows, s_rows2, r_rows2, s_mate, r_mate, s_cross, r_cross,
-    s_map, r_map, s_map2, r_map2,
+    s_map, r_map, s_map2, r_map2, s_blocks, r_blocks, s_blocks2, r_blocks2, s_load,
+    field_ref, weight_ref, probe_ref,
 ):
+    loads = [
+        pltpu.make_async_copy(source, target, s_load.at[k])
+        for k, (source, target) in enumerate(
+            ((field_any, field_ref), (weight_any, weight_ref), (probe_any, probe_ref))
+        )
+    ]
+    for load in loads:
+        load.start()
     d = lax.axis_index("dp")
     c = lax.axis_index("chan")
     rows, width = field_ref.shape
@@ -250,8 +317,12 @@
             barrier, inc=1, device_id={"chan": lax.rem(c + j, nc)}, device_id_type=pl.DeviceIdType.MESH
         )
 
+    big_ref[...] = jnp.zeros((size, size), F32)
+    loads[0].wait()
+    loads[1].wait()
     conv_into(field_ref, weight_ref, pad_ref, resp_ref)
     responses = resp_ref[...]
+    loads[2].wait()
     for j in range(nc):
         block = dot_bf16(responses, probe_ref[:, j * share : (j + 1) * share], ((1,), (0,)))
         part_ref[j] = block.astype(BF16)
@@ -260,7 +331,6 @@
     started = exchange(
         "chan", c, nc, lambda j, p: part_ref.at[p], lambda j, p: part_in_ref.at[j], s_part, r_part
     )
-    big_ref[...] = jnp.zeros((size, size), F32)
     arrived("chan", c, nc, lambda j, p: part_in_ref.at[j], s_part, r_part)
     mine = part_ref[c].astype(F32)
     for j in range(1, nc):
@@ -291,12 +361,22 @@
     for j in range(1, nd):
         total = total + gin_ref[j]
     gsum_ref[c, d] = total
-    started += gather("dp", d, nd, lambda i: gsum_ref.at[c, i], s_rows, r_rows, s_rows2, r_rows2)
-    started.append(
-        send("dp", mate, cpart_ref.at[1 - low], cmate_ref, s_mate.at[0], r_mate.at[0])
-    )
-    started += gather(
-        "chan", c, nc, lambda i: gsum_ref.at[i], s_blocks, r_blocks, s_blocks2, r_blocks2
+    places = [lax.rem(high + j, pairs) for j in range(1, pairs)] + [high]
+
+    def middle():
+        for j, place in enumerate(places):
+            started.append(
+                send("dp", mate, cpart_ref.at[1 - low, place], cmate_ref.at[place], s_mate.at[j], r_mate.at[j])
+            )
+
+    def add_mate(j):
+        place = places[j]
+        expect("dp", mate, cmate_ref.at[place], s_mate.at[j], r_mate.at[j])
+        cmate_ref[place] = cmate_ref[place] + cpart_ref[low, place]
+
+    started += gather_rows(
+        d, nd, c, nc, lambda k, i: gsum_ref.at[k, i],
+        (s_rows, r_rows), (s_rows2, r_rows2), (s_blocks, r_blocks), (s_blocks2, r_blocks2), middle,
     )
     for first in range(nc):
         for k in range(half + 1):
@@ -321,19 +401,24 @@
         above = lax.broadcasted_iota(jnp.int32, square, 1) > lax.broadcasted_iota(jnp.int32, square, 0)
         big_ref[...] = jnp.where(above, full, jnp.transpose(full))
 
-    def between():
-        expect("dp", mate, cmate_ref, s_mate.at[0], r_mate.at[0])
-        cmate_ref[...] = cmate_ref[...] + cpart_ref[low]
-        for j in range(1, pairs):
-            place = lax.rem(high + j, pairs)
-            send("dp", 2 * place + low, cmate_ref.at[place], cin_ref.at[j], s_cross.at[j], r_cross.at[j])
-
+    def pass_on(first, end):
+        for j in range(first, end):
+            add_mate(j)
+            place = places[j]
+            send(
+                "dp", 2 * place + low, cmate_ref.at[place], cin_ref.at[j + 1],
+                s_cross.at[j + 1], r_cross.at[j + 1],
+            )
+
+    early = pairs // 2
+    between = (lambda: pass_on(0, early), lambda: pass_on(early, pairs - 1))
     eliminate(big_ref, work_ref, stack_ref, diag_ref, size, between)
     square = (size, size)
     row_of = lax.broadcasted_iota(jnp.int32, square, 0)
     lane_of = lax.broadcasted_iota(jnp.int32, square, 1)
     inverse = jnp.where(lane_of <= row_of, big_ref[...], 0.0)
     ih, im, il = split3(inverse)
+    add_mate(pairs - 1)
     own = cmate_ref[high]
     for j in range(1, pairs):
         sender = 2 * lax.rem(high + pairs - j, pairs) + low
@@ -400,6 +485,7 @@
     return pl.pallas_call(
         functools.partial(last_kernel if last else first_kernel, nd, nc, rows * nd),
         out_shape=(restored, upper) if last else restored,
+        in_specs=[pl.BlockSpec(memory_space=pl.ANY)] * 3,
         scratch_shapes=[
             pltpu.VMEM((rows + 2 * PAD, width), F32),
             pltpu.VMEM((padded, width), BF16),
@@ -418,8 +504,15 @@
             pltpu.VMEM((6 * BLOCK, size), BF16),
             pltpu.VMEM((size // BLOCK, BLOCK, BLOCK), F32),
         ]
-        + [chan_sems] * 10
-        + [dp_sems] * 14,
+        + [chan_sems] * 6
+        + [dp_sems] * 14
+        + [pltpu.SemaphoreType.DMA((nd, nc // 2))] * 4
+        + [
+            pltpu.SemaphoreType.DMA((3,)),
+            pltpu.VMEM(field.shape, BF16),
+            pltpu.VMEM(weight.shape, BF16),
+            pltpu.VMEM(probe.shape, BF16),
+        ],
         compiler_params=pltpu.CompilerParams(
             vmem_limit_bytes=VMEM_LIMIT, collective_id=1 if last else 0, has_side_effects=True
         ),

time: 145 us -> 145 us (level)
  no operation moved by 1% of the time
where the time goes in v4:
time: 145 us
  Pallas kernels  140 us (97%)
  local copies, waits for them, and re-layouts  4.72 us (3%)
    pallas_call x2, Pallas kernels, layer(): pl.pallas_call(functools.partial(last_kernel if last else first_kernel, n...  140 us
    unnamed x12, local copies, waits for them, and re-layouts  4.72 us

profile of v4, /device:TPU:0, one launch (start us, length us, event | category | flops | bytes accessed | tf_op | source)
XLA Modules:
  0.0 145.0 jit_solution(18430183530979276990)
XLA Ops:
  0.6 0.0 copy-start
  0.6 1.0 copy-done
  1.7 0.0 copy-start.2
  1.7 1.0 copy-done.2
  2.7 0.0 copy-start.3
  2.7 1.0 copy-done.3
  3.6 0.0 copy-start.1
  3.6 0.0 copy-start.4
  3.6 71.7 %shard_map.68.refs_0_ = bf16[392,512]{1,0:T(8,128)(2,1)S(1)} custom-call(bf16[392,512]{1,0:T(8,128)(2,1)S(1)} %copy-done.2, bf16[9,32,512]{2,1,0:T(8,128)(2,1)S(1)} %copy-done.3, bf16[512,512]{1,0:T(8,128)(2,1)S(1)} %copy-done), custom_call_target="tpu_custom_call" | custom-call | tf_op jit(solution)/shard_map/pallas_call | solution.py:485
  75.3 0.0 copy-done.1
  75.3 0.0 copy-done.4
  75.3 67.9 %shard_map.69 = (bf16[392,512]{1,0:T(8,128)(2,1)S(1)}, f32[512,512]{1,0:T(8,128)S(1)}) custom-call(bf16[392,512]{1,0:T(8,128)(2,1)S(1)} %shard_map.68.refs_0_, bf16[9,32,512]{2,1,0:T(8,128)(2,1)S(1)} %copy-done.4, bf16[512,512]{1,0:T(8,128)(2,1)S(1)} %copy-done.1), custom_call_target="tpu_custom_call" | custom-call | tf_op jit(solution)/shard_map/pallas_call | solution.py:485
  143.3 0.8 copy.9
  144.0 1.0 copy.10
Async XLA Ops:
  0.6 1.0 copy-start
  1.7 1.0 copy-start.2
  2.7 1.0 copy-start.3
  3.6 71.7 %copy-start.1 = (bf16[512,512]{1,0:T(8,128)(2,1)S(1)}, bf16[512,512]{1,0:T(8,128)(2,1)}, u32[]{:S(2)}) copy-start(bf16[512,512]{1,0:T(8,128)(2,1)} %refs_2_.1) | copy-start | bytes 1572868
  3.6 71.7 %copy-start.4 = (bf16[9,32,512]{2,1,0:T(8,128)(2,1)S(1)}, bf16[9,32,512]{2,1,0:T(8,128)(2,1)}, u32[]{:S(2)}) copy-start(bf16[9,32,512]{2,1,0:T(8,128)(2,1)} %refs_1_.1) | copy-start | bytes 884740

commit v5 on v4

--- a/solution.py
+++ b/solution.py
@@ -120,7 +120,7 @@
             work_ref[rest:BLOCK, :] = work_ref[rest:BLOCK, :] - update[rest:BLOCK, :]
 
 
-def eliminate(big_ref, work_ref, stack_ref, diag_ref, size, between):
+def eliminate(big_ref, work_ref, stack_ref, diag_ref, size):
     blocks = size // BLOCK
     square = (BLOCK, BLOCK)
     eye = jnp.where(
@@ -131,8 +131,6 @@
 
     @pl.loop(0, blocks)
     def _(b):
-        for step, task in enumerate(between):
-            pl.when(b == step + 1)(task)
         at = pl.ds(pl.multiple_of(b * BLOCK, BLOCK), BLOCK)
         work_ref[:, 0:BLOCK] = big_ref[at, at]
         work_ref[:, BLOCK : 2 * BLOCK] = eye
@@ -226,7 +224,7 @@
     return copies
 
 
-def gather_rows(d, nd, c, nc, slot, far, mate_sems, chan_far, chan_mate, middle):
+def gather_rows(d, nd, c, nc, slot, far, mate_sems, chan_far, chan_mate):
     high, low = d // 2, d % 2
     mate = d + 1 - 2 * low
     pairs = nd // 2
@@ -262,7 +260,6 @@
         expect("dp", mate, slot(c, origin), mate_sems[0].at[j], mate_sems[1].at[j])
         over_chan(2 * j + 1, origin)
         pieces.append(origin)
-    middle()
     for order, piece in enumerate(pieces):
         for j in range(1, chan_pairs):
             sender = 2 * lax.rem(chan_high + chan_pairs - j, chan_pairs) + chan_low
@@ -356,19 +353,17 @@
     cross = dot_bf16(responses, sketch, ((0,), (0,)))
     for j in range(nd):
         cpart_ref[j % 2, j // 2] = cross[j * cross_rows : (j + 1) * cross_rows, :]
+    places = [lax.rem(high + j, pairs) for j in range(1, pairs)] + [high]
+
+    for j, place in enumerate(places):
+        started.append(
+            send("dp", mate, cpart_ref.at[1 - low, place], cmate_ref.at[place], s_mate.at[j], r_mate.at[j])
+        )
     arrived("dp", d, nd, lambda j, p: gin_ref.at[j], s_gram, r_gram)
     total = gpart_ref[d]
     for j in range(1, nd):
         total = total + gin_ref[j]
     gsum_ref[c, d] = total
-    places = [lax.rem(high + j, pairs) for j in range(1, pairs)] + [high]
-
-    def middle():
-        for j, place in enumerate(places):
-            started.append(
-                send("dp", mate, cpart_ref.at[1 - low, place], cmate_ref.at[place], s_mate.at[j], r_mate.at[j])
-            )
-
     def add_mate(j):
         place = places[j]
         expect("dp", mate, cmate_ref.at[place], s_mate.at[j], r_mate.at[j])
@@ -376,7 +371,7 @@
 
     started += gather_rows(
         d, nd, c, nc, lambda k, i: gsum_ref.at[k, i],
-        (s_rows, r_rows), (s_rows2, r_rows2), (s_blocks, r_blocks), (s_blocks2, r_blocks2), middle,
+        (s_rows, r_rows), (s_rows2, r_rows2), (s_blocks, r_blocks), (s_blocks2, r_blocks2),
     )
     for first in range(nc):
         for k in range(half + 1):
@@ -410,9 +405,8 @@
                 s_cross.at[j + 1], r_cross.at[j + 1],
             )
 
-    early = pairs // 2
-    between = (lambda: pass_on(0, early), lambda: pass_on(early, pairs - 1))
-    eliminate(big_ref, work_ref, stack_ref, diag_ref, size, between)
+    pass_on(0, pairs - 1)
+    eliminate(big_ref, work_ref, stack_ref, diag_ref, size)
     square = (size, size)
     row_of = lax.broadcasted_iota(jnp.int32, square, 0)
     lane_of = lax.broadcasted_iota(jnp.int32, square, 1)

time: 145 us -> 157 us (1.083)
  Pallas kernels: 140 us -> 151 us
    pallas_call x2, Pallas kernels: 140 us -> 151 us  [layer(): pl.pallas_call(functools.partial(last_kernel if last else first_kernel, n...]
where the time goes in v5:
time: 157 us; the launch traced here: 156 us
  Pallas kernels  151 us (96%)
  local copies, waits for them, and re-layouts  4.72 us (3%)
    pallas_call x2, Pallas kernels, layer(): pl.pallas_call(functools.partial(last_kernel if last else first_kernel, n...  151 us
    unnamed x12, local copies, waits for them, and re-layouts  4.72 us

profile of v5, /device:TPU:0, one launch (start us, length us, event | category | flops | bytes accessed | tf_op | source)
XLA Modules:
  0.0 156.5 jit_solution(15144461712314668249)
XLA Ops:
  0.6 0.0 copy-start
  0.6 1.0 copy-done
  1.7 0.0 copy-start.2
  1.7 1.0 copy-done.2
  2.7 0.0 copy-start.3
  2.7 1.0 copy-done.3
  3.6 0.0 copy-start.1
  3.6 0.0 copy-start.4
  3.6 77.0 %shard_map.68.refs_0_ = bf16[392,512]{1,0:T(8,128)(2,1)S(1)} custom-call(bf16[392,512]{1,0:T(8,128)(2,1)S(1)} %copy-done.2, bf16[9,32,512]{2,1,0:T(8,128)(2,1)S(1)} %copy-done.3, bf16[512,512]{1,0:T(8,128)(2,1)S(1)} %copy-done), custom_call_target="tpu_custom_call" | custom-call | tf_op jit(solution)/shard_map/pallas_call | solution.py:479
  80.6 0.0 copy-done.1
  80.7 0.0 copy-done.4
  80.7 74.1 %shard_map.69 = (bf16[392,512]{1,0:T(8,128)(2,1)S(1)}, f32[512,512]{1,0:T(8,128)S(1)}) custom-call(bf16[392,512]{1,0:T(8,128)(2,1)S(1)} %shard_map.68.refs_0_, bf16[9,32,512]{2,1,0:T(8,128)(2,1)S(1)} %copy-done.4, bf16[512,512]{1,0:T(8,128)(2,1)S(1)} %copy-done.1), custom_call_target="tpu_custom_call" | custom-call | tf_op jit(solution)/shard_map/pallas_call | solution.py:479
  154.8 0.8 copy.9
  155.5 1.0 copy.10
Async XLA Ops:
  0.6 1.0 copy-start
  1.7 1.0 copy-start.2
  2.7 1.0 copy-start.3
  3.6 77.0 %copy-start.1 = (bf16[512,512]{1,0:T(8,128)(2,1)S(1)}, bf16[512,512]{1,0:T(8,128)(2,1)}, u32[]{:S(2)}) copy-start(bf16[512,512]{1,0:T(8,128)(2,1)} %refs_2_.1) | copy-start | bytes 1572868
  3.6 77.0 %copy-start.4 = (bf16[9,32,512]{2,1,0:T(8,128)(2,1)S(1)}, bf16[9,32,512]{2,1,0:T(8,128)(2,1)}, u32[]{:S(2)}) copy-start(bf16[9,32,512]{2,1,0:T(8,128)(2,1)} %refs_1_.1) | copy-start | bytes 884740

commit v6 on v4

--- a/solution.py
+++ b/solution.py
@@ -92,31 +92,36 @@
         cols = [
             jnp.broadcast_to(left[:, top + k : top + k + 1], (PANEL, BLOCK)) for k in range(PANEL)
         ]
-        scale = jnp.zeros((PANEL, BLOCK), F32)
+        rest = top + PANEL
+        if rest < BLOCK:
+            before = stack_first(work_ref[:, top:rest], 1)
+        upper_left, upper_right = jnp.zeros_like(left), jnp.zeros_like(right)
+        inverse_of = jnp.zeros_like(left)
         for i in range(PANEL):
             pivot = jnp.broadcast_to(cols[i][i : i + 1, :], (PANEL, BLOCK))
             root = lax.rsqrt(pivot)
-            scale = jnp.where(row_of == i, root, scale)
-            if i < PANEL - 1:
-                below = jnp.where(row_of > i, cols[i], 0.0)
-                ahead = below * cols[i + 1][i : i + 1, :]
-                square = root * root
-                cols[i + 1] = cols[i + 1] - ahead * square
-                factor = below * square
-                for k in range(i + 2, PANEL):
-                    cols[k] = cols[k] - factor * cols[k][i : i + 1, :]
-                left = left - factor * left[i : i + 1, :]
-                right = right - factor * right[i : i + 1, :]
-        left = left * scale
-        right = right * scale
+            square = root * root
+            here = row_of == i
+            inverse_of = jnp.where(here, square, inverse_of)
+            left_row, right_row = left[i : i + 1, :], right[i : i + 1, :]
+            upper_left = jnp.where(here, left_row * root, upper_left)
+            upper_right = jnp.where(here, right_row * root, upper_right)
+            others = jnp.where(here, 0.0, cols[i])
+            if i + 1 < PANEL:
+                cols[i + 1] = cols[i + 1] - (others * cols[i + 1][i : i + 1, :]) * square
+            factor = others * square
+            for k in range(i + 2, PANEL):
+                cols[k] = cols[k] - factor * cols[k][i : i + 1, :]
+            left = left - factor * left_row
+            right = right - factor * right_row
         lane_of = lax.broadcasted_iota(jnp.int32, (PANEL, BLOCK), 1)
-        left = jnp.where(lane_of >= top + row_of, left, 0.0)
-        work_ref[top : top + PANEL, 0:BLOCK] = left
-        work_ref[top : top + PANEL, BLOCK : 2 * BLOCK] = right
-        if top + PANEL < BLOCK:
-            rest = top + PANEL
-            second = jnp.concatenate([stack_second(left), stack_second(right)], axis=1)
-            update = dot_bf16(stack_first(left, 0), second, ((0,), (0,)))
+        work_ref[top:rest, 0:BLOCK] = jnp.where(lane_of >= top + row_of, upper_left, 0.0)
+        work_ref[top:rest, BLOCK : 2 * BLOCK] = upper_right
+        if rest < BLOCK:
+            second = jnp.concatenate(
+                [stack_second(left * inverse_of), stack_second(right * inverse_of)], axis=1
+            )
+            update = dot_bf16(before, second, ((1,), (0,)))
             work_ref[rest:BLOCK, :] = work_ref[rest:BLOCK, :] - update[rest:BLOCK, :]
 
 

time: 145 us -> 144 us (level)
  no operation moved by 1% of the time
where the time goes in v6:
time: 144 us
  Pallas kernels  139 us (97%)
  local copies, waits for them, and re-layouts  4.72 us (3%)
    pallas_call x2, Pallas kernels, layer(): pl.pallas_call(functools.partial(last_kernel if last else first_kernel, n...  139 us
    unnamed x12, local copies, waits for them, and re-layouts  4.72 us

profile of v6, /device:TPU:0, one launch (start us, length us, event | category | flops | bytes accessed | tf_op | source)
XLA Modules:
  0.0 144.0 jit_solution(15305244461616168653)
XLA Ops:
  0.6 0.0 copy-start
  0.6 1.0 copy-done
  1.7 0.0 copy-start.2
  1.7 1.0 copy-done.2
  2.7 0.0 copy-start.3
  2.7 1.0 copy-done.3
  3.6 0.0 copy-start.1
  3.6 0.0 copy-start.4
  3.6 70.7 %shard_map.68.refs_0_ = bf16[392,512]{1,0:T(8,128)(2,1)S(1)} custom-call(bf16[392,512]{1,0:T(8,128)(2,1)S(1)} %copy-done.2, bf16[9,32,512]{2,1,0:T(8,128)(2,1)S(1)} %copy-done.3, bf16[512,512]{1,0:T(8,128)(2,1)S(1)} %copy-done), custom_call_target="tpu_custom_call" | custom-call | tf_op jit(solution)/shard_map/pallas_call | solution.py:490
  74.3 0.0 copy-done.1
  74.3 0.0 copy-done.4
  74.3 68.0 %shard_map.69 = (bf16[392,512]{1,0:T(8,128)(2,1)S(1)}, f32[512,512]{1,0:T(8,128)S(1)}) custom-call(bf16[392,512]{1,0:T(8,128)(2,1)S(1)} %shard_map.68.refs_0_, bf16[9,32,512]{2,1,0:T(8,128)(2,1)S(1)} %copy-done.4, bf16[512,512]{1,0:T(8,128)(2,1)S(1)} %copy-done.1), custom_call_target="tpu_custom_call" | custom-call | tf_op jit(solution)/shard_map/pallas_call | solution.py:490
  142.3 0.8 copy.9
  143.0 1.0 copy.10
Async XLA Ops:
  0.6 1.0 copy-start
  1.7 1.0 copy-start.2
  2.7 1.0 copy-start.3
  3.6 70.7 %copy-start.1 = (bf16[512,512]{1,0:T(8,128)(2,1)S(1)}, bf16[512,512]{1,0:T(8,128)(2,1)}, u32[]{:S(2)}) copy-start(bf16[512,512]{1,0:T(8,128)(2,1)} %refs_2_.1) | copy-start | bytes 1572868
  3.6 70.7 %copy-start.4 = (bf16[9,32,512]{2,1,0:T(8,128)(2,1)S(1)}, bf16[9,32,512]{2,1,0:T(8,128)(2,1)}, u32[]{:S(2)}) copy-start(bf16[9,32,512]{2,1,0:T(8,128)(2,1)} %refs_1_.1) | copy-start | bytes 884740
